TPU v7x, 32 devices: a whole 2x2x4 slice. The times are simulated.
32 devices in a mesh: parts: 2 (over x), sta: 16 (over z, y, core).
Axes of the slice: x: 2, y: 2, z: 4, core: 2. Of those that a mesh axis runs over, the one named last changes fastest.
Arguments:
- raw_traces: bfloat16 [512, 16384], P('parts', 'sta'), parts along dimension 0, may hold values from -6 to 6
- filter_taps: bfloat16 [256], replicated, may hold values from -0.375 to 0.375
- station_order: int32 [512], P('parts'), parts along dimension 0, may hold values from 0 to 255, each once
- window_starts: int32 [32], P('parts'), parts along dimension 0, may hold values from 0 to 2048, as said below
- pairing: int32 [4, 16], replicated, may hold values from 0 to 15, as said below
Outputs:
- correlation: float32 [4, 512, 16, 256], P(None, ('parts', 'sta')), parts along dimension 1
There are 2 independent parts, one for each index of `parts`. A program takes and returns all parts, laid end to end along the dimension named above; an argument that names none is the same for every part. Nothing has to cross between parts.
Inputs may be any that keep to these rules, and one draw needn't show every extreme that they name: Each station appears once; block b holds the stations station_order[b * 16 + j], j < 16. `window_starts`: starts never fall; the first is 0 and the last is 2048; consecutive starts differ by at most 273. Row r is one round of a single round-robin tournament over the 16 blocks: pairing[r, pairing[r, b]] = b, pairing[r, b] != b, and no two rows pair the same two blocks.
All inputs are finite; a program needn't handle non-finite values.
Results may differ from a plain program's by a relative error of at most 0.0049.
Values may be sent and summed in bfloat16 or wider, within the bound.
A program may use at most 128 MiB of HBM per device.

v0:
```python
import functools
import math

import jax
import jax.numpy as jnp
import ml_dtypes
import numpy as np
from jax import lax
from jax.experimental import pallas as pl
from jax.experimental.pallas import tpu as pltpu
from jax.sharding import PartitionSpec as P

SB = 16
DEC = 4
TAPS = 256
SEG = 2048
BAND = 64
LAGS = 256
ROUNDS = 4
BINS = 1024
LANE = 128
SPAN = LANE * DEC + TAPS
GROUPS = ROUNDS + 1
ROWS = GROUPS * SB
FT = 128
TILES = BINS // FT
QUAD = 4
MESH = pl.DeviceIdType.MESH


def dft_tiles():
    sample = np.arange(SEG)
    frequency = np.arange(BINS)
    angles = (sample[:, None] * frequency[None, :] % SEG) * (2.0 * math.pi / SEG)
    taper = (0.5 - 0.5 * np.cos(sample * (2.0 * math.pi / SEG)))[:, None]
    both = np.stack([np.cos(angles) * taper, -np.sin(angles) * taper], axis=1)
    both = both.reshape(SEG, 2, TILES, FT).transpose(2, 0, 1, 3).reshape(TILES, SEG, 2 * FT)
    return both.astype(np.float32).astype(ml_dtypes.bfloat16)


def lag_tiles(window_count):
    frequency = np.arange(BINS)
    offset = np.arange(LAGS) - LAGS // 2 + SEG
    angles = (frequency[:, None] * offset[None, :] % SEG) * (2.0 * math.pi / SEG)
    scale = 1.0 / math.sqrt(BINS * window_count)
    both = np.stack([np.cos(angles) * scale, -np.sin(angles) * scale])
    both = both.reshape(2, TILES, FT, LAGS).transpose(1, 0, 2, 3).reshape(TILES, 2 * FT, LAGS)
    return both.astype(np.float32).astype(ml_dtypes.bfloat16)


def band_ones():
    same = np.arange(FT)[:, None] // BAND == np.arange(FT)[None, :] // BAND
    return np.concatenate([same, same]).astype(ml_dtypes.bfloat16)


def gather_kernel(members, raw_ref, taps_ref, order_ref, out_ref, halo, low, halo_sems, own_sem, send_sems, recv_sems):
    me = lax.axis_index("sta")
    stations, local_time = raw_ref.shape
    line = members // QUAD
    rank, lead = me // QUAD, me % QUAD
    far = [lax.rem(rank + k, line) * QUAD + lead for k in range(1, line)]
    across = rank * QUAD + lax.rem(lead + 2, QUAD)
    twin = me + 1 - 2 * lax.rem(me, 2)
    after, before = lax.rem(me + 1, members), lax.rem(me + members - 1, members)

    barrier = pltpu.get_barrier_semaphore()
    greeted = far + [across, twin, after, before]
    for peer in greeted:
        pl.semaphore_signal(barrier, inc=1, device_id={"sta": peer}, device_id_type=MESH)
    pl.semaphore_wait(barrier, len(greeted))

    halo_copy = pltpu.make_async_remote_copy(
        src_ref=raw_ref.at[:, local_time - TAPS :],
        dst_ref=halo,
        send_sem=halo_sems.at[0],
        recv_sem=halo_sems.at[1],
        device_id={"sta": after},
        device_id_type=MESH,
    )

    @pl.when(me < members - 1)
    def _():
        halo_copy.start()

    banded = jnp.broadcast_to(taps_ref[...], (LANE, SPAN))
    banded = pltpu.roll(banded, 0, 1, stride=DEC, stride_axis=0).astype(jnp.bfloat16)
    picks = (lax.broadcasted_iota(jnp.int32, (stations, stations), 1) == order_ref[...]).astype(
        jnp.float32
    ).astype(jnp.bfloat16)
    dims = (((1,), (1,)), ((), ()))

    def filtered(piece, samples):
        summed = lax.dot_general(samples, banded, dims, preferred_element_type=jnp.float32)
        ordered = jnp.dot(picks, summed.astype(jnp.bfloat16), preferred_element_type=jnp.float32)
        low[piece] = ordered.astype(jnp.bfloat16)

    for piece in range(1, low.shape[0]):
        first = piece * LANE * DEC - TAPS
        filtered(piece, raw_ref[:, first : first + SPAN])

    @pl.when(me > 0)
    def _():
        halo_copy.wait_recv()

    @pl.when(me == 0)
    def _():
        halo[...] = jnp.zeros_like(halo)

    filtered(0, jnp.concatenate([halo[...], raw_ref[:, : LANE * DEC]], axis=1))

    sent = []

    def send(source, slot, peer):
        n = len(sent)
        copy = pltpu.make_async_remote_copy(
            src_ref=source,
            dst_ref=out_ref.at[slot],
            send_sem=send_sems.at[n],
            recv_sem=recv_sems.at[slot],
            device_id={"sta": peer},
            device_id_type=MESH,
        )
        copy.start()
        sent.append(copy)

    def arrived(slot):
        pltpu.make_async_remote_copy(
            src_ref=low,
            dst_ref=out_ref.at[slot],
            send_sem=send_sems.at[0],
            recv_sem=recv_sems.at[slot],
            device_id={"sta": twin},
            device_id_type=MESH,
        ).wait_recv()

    order = sorted(range(line - 1), key=lambda k: min(k + 1, line - 1 - k))
    for k in order:
        send(low, me, far[k])
    send(low, me, across)
    send(low, me, twin)
    own = pltpu.make_async_copy(low, out_ref.at[me], own_sem)
    own.start()
    shift = across - me
    arrived(me + shift)
    send(out_ref.at[me + shift], me + shift, twin)
    for k in order:
        arrived(far[k])
        send(out_ref.at[far[k]], far[k], across)
        send(out_ref.at[far[k]], far[k], twin)
    for k in order:
        arrived(far[k] + shift)
        send(out_ref.at[far[k] + shift], far[k] + shift, twin)
    turn = twin - me
    for slot in [me] + [far[k] for k in order]:
        arrived(slot + turn)
        arrived(slot + shift + turn)
    own.wait()
    for copy in sent:
        copy.wait_send()

    @pl.when(me < members - 1)
    def _():
        halo_copy.wait_send()


def correlate_kernel(
    starts_ref, groups_ref, low_ref, dft_ref, lag_ref, ones_ref, out_ref, rows, windows, white, cross, sems
):
    tile = pl.program_id(0)
    planes = low_ref.shape[0]
    window_count = starts_ref.shape[0]

    @pl.when(tile == 0)
    def _():
        copies = []
        for g in range(GROUPS):
            first = pl.multiple_of(groups_ref[g] * SB, SB)
            copy = pltpu.make_async_copy(
                low_ref.at[:, pl.ds(first, SB), :],
                rows.at[pl.ds(0, planes), pl.ds(g * SB, SB), :],
                sems.at[g],
            )
            copy.start()
            copies.append(copy)
        rows[planes] = jnp.zeros((ROWS, LANE), jnp.bfloat16)
        for copy in copies:
            copy.wait()
        lane = lax.broadcasted_iota(jnp.int32, (ROWS, LANE), 1)

        def one_window(w, carry):
            start = starts_ref[w]
            plane = start // LANE
            left = LANE - start % LANE
            back = left % LANE
            now = pltpu.roll(rows[plane].astype(jnp.float32), back, 1)
            for piece in range(SEG // LANE):
                later = pltpu.roll(rows[plane + piece + 1].astype(jnp.float32), back, 1)
                windows[
                    pl.ds(pl.multiple_of(w * ROWS, SB), ROWS), piece * LANE : (piece + 1) * LANE
                ] = jnp.where(lane < left, now, later).astype(jnp.bfloat16)
                now = later
            return carry

        lax.fori_loop(0, window_count, one_window, 0)
        out_ref[...] = jnp.zeros_like(out_ref)

    per_chunk = 8

    def one_chunk(n, carry):
        chunk = windows[pl.ds(pl.multiple_of(n * per_chunk * ROWS, SB), per_chunk * ROWS), :]
        spectrum = jnp.dot(chunk, dft_ref[0], preferred_element_type=jnp.float32)
        real, imag = spectrum[:, :FT], spectrum[:, FT:]
        power = real * real + imag * imag
        high = power.astype(jnp.bfloat16)
        low = (power - high.astype(jnp.float32)).astype(jnp.bfloat16)
        level = jnp.dot(
            jnp.concatenate([high, low], axis=1), ones_ref[...], preferred_element_type=jnp.float32
        )
        scale = lax.rsqrt(level * (1.0 / (2 * BAND)) + 1e-06)
        for c, part in enumerate((real, imag)):
            rounded = (part * scale).astype(jnp.bfloat16).astype(jnp.float32)
            white[c, pl.ds(n * per_chunk, per_chunk)] = rounded.reshape(per_chunk, ROWS, FT)
        return carry

    lax.fori_loop(0, window_count // per_chunk, one_chunk, 0)

    pair = 2

    def one_pair(n, carry):
        re = [[jnp.zeros((SB, FT), jnp.float32)] * ROUNDS for _ in range(pair)]
        im = [[jnp.zeros((SB, FT), jnp.float32)] * ROUNDS for _ in range(pair)]
        for w in range(window_count):
            own = [
                [
                    jnp.broadcast_to(white[c, w, pl.ds(n * pair + p, 1), :], (SB, FT))
                    for c in range(2)
                ]
                for p in range(pair)
            ]
            for r in range(ROUNDS):
                theirs = [white[c, w, (r + 1) * SB : (r + 2) * SB, :] for c in range(2)]
                for p in range(pair):
                    re[p][r] = re[p][r] + own[p][0] * theirs[0] + own[p][1] * theirs[1]
                    im[p][r] = im[p][r] + own[p][1] * theirs[0] - own[p][0] * theirs[1]
        for p in range(pair):
            for r in range(ROUNDS):
                at = pl.ds(pl.multiple_of((n * pair + p) * SB, SB), SB)
                cross[r, at, :FT] = re[p][r].astype(jnp.bfloat16)
                cross[r, at, FT:] = im[p][r].astype(jnp.bfloat16)
        return carry

    lax.fori_loop(0, SB // pair, one_pair, 0)
    for r in range(ROUNDS):
        out_ref[r] += jnp.dot(cross[r], lag_ref[0], preferred_element_type=jnp.float32)


def correlate(window_starts, groups, low, dft, lag, ones):
    window_count = window_starts.shape[0]
    planes = low.shape[0]
    grid_spec = pltpu.PrefetchScalarGridSpec(
        num_scalar_prefetch=2,
        grid=(TILES,),
        in_specs=[
            pl.BlockSpec(memory_space=pl.ANY),
            pl.BlockSpec((1, SEG, 2 * FT), lambda n, *_: (n, 0, 0)),
            pl.BlockSpec((1, 2 * FT, LAGS), lambda n, *_: (n, 0, 0)),
            pl.BlockSpec((2 * FT, FT), lambda n, *_: (0, 0)),
        ],
        out_specs=pl.BlockSpec((ROUNDS, SB * SB, LAGS), lambda n, *_: (0, 0, 0)),
        scratch_shapes=[
            pltpu.VMEM((planes + 1, ROWS, LANE), jnp.bfloat16),
            pltpu.VMEM((window_count * ROWS, SEG), jnp.bfloat16),
            pltpu.VMEM((2, window_count, ROWS, FT), jnp.float32),
            pltpu.VMEM((ROUNDS, SB * SB, 2 * FT), jnp.bfloat16),
            pltpu.SemaphoreType.DMA((GROUPS,)),
        ],
    )
    return pl.pallas_call(
        correlate_kernel,
        grid_spec=grid_spec,
        out_shape=jax.ShapeDtypeStruct((ROUNDS, SB * SB, LAGS), jnp.float32),
        compiler_params=pltpu.CompilerParams(vmem_limit_bytes=48 * 2**20),
    )(window_starts, groups, low, dft, lag, ones)


def body(raw_traces, filter_taps, station_order, window_starts, pairing):
    members = lax.axis_size("sta")
    me = lax.axis_index("sta")
    stations, local_time = raw_traces.shape
    window_count = window_starts.shape[0]
    pieces = local_time // (LANE * DEC)
    taps = jnp.pad(filter_taps.astype(jnp.float32)[::-1], (DEC, SPAN - TAPS - DEC)).reshape(1, SPAN)
    in_vmem = pl.BlockSpec(memory_space=pltpu.VMEM)
    low = pl.pallas_call(
        functools.partial(gather_kernel, members),
        out_shape=jax.ShapeDtypeStruct((members, pieces, stations, LANE), jnp.bfloat16),
        in_specs=[in_vmem] * 3,
        out_specs=pl.BlockSpec(memory_space=pl.ANY),
        scratch_shapes=[
            pltpu.VMEM((stations, TAPS), jnp.bfloat16),
            pltpu.VMEM((pieces, stations, LANE), jnp.bfloat16),
            pltpu.SemaphoreType.DMA((2,)),
            pltpu.SemaphoreType.DMA,
            pltpu.SemaphoreType.DMA((members,)),
            pltpu.SemaphoreType.DMA((members,)),
        ],
        compiler_params=pltpu.CompilerParams(
            collective_id=0, has_side_effects=True, vmem_limit_bytes=40 * 2**20
        ),
    )(raw_traces, taps, station_order.reshape(stations, 1))
    low = low.reshape(members * pieces, stations, LANE)
    groups = jnp.concatenate([me[None].astype(jnp.int32), lax.dynamic_slice_in_dim(pairing, me, 1, 1)[:, 0]])
    correlated = correlate(
        window_starts,
        groups,
        low,
        jnp.asarray(dft_tiles()),
        jnp.asarray(lag_tiles(window_count)),
        jnp.asarray(band_ones()),
    )
    return correlated.reshape(ROUNDS, SB, SB, LAGS)


def solution(mesh):
    return jax.shard_map(
        body,
        mesh=mesh,
        in_specs=(P("parts", "sta"), P(), P("parts"), P("parts"), P()),
        out_specs=P(None, ("parts", "sta"), None, None),
        check_vma=False,
    )
```

profile of v0, /device:TPU:0, one launch (start us, length us, event | category | flops | bytes accessed | tf_op | source)
XLA Modules:
  0.0 75.4 jit_solution(6330560864976787900)
XLA Ops:
  0.0 0.0 copy-start
  0.0 0.7 copy-done
  0.7 0.2 dynamic-slice_reduce_fusion
  0.9 0.1 pad_add_fusion.groups_ref
  0.9 0.7 rev.3
  1.7 0.1 pad.4
  1.8 0.8 %copy.9.order_ref = s32[256,1]{1,0:T(8,128)S(1)} copy(s32[256,1]{0,1:T(1,128)} %bitcast.5) | data formatting | bytes 2048 | tf_op jit(solution)/shard_map/reshape | solution.py:310
  2.6 0.0 copy-start.2
  2.6 1.0 %copy-done.2 = bf16[256,1024]{1,0:T(8,128)(2,1)S(1)} copy-done((bf16[256,1024]{1,0:T(8,128)(2,1)S(1)}, bf16[256,1024]{1,0:T(8,128)(2,1)}, u32[]{:S(2)}) %copy-start.2) | copy-done | bytes 524312
  3.6 25.3 %shard_map.82 = bf16[16,2,256,128]{3,2,1,0:T(8,128)(2,1)S(1)} custom-call(bf16[256,1024]{1,0:T(8,128)(2,1)S(1)} %copy-done.2, f32[1,768]{1,0:T(1,128)S(1)} %reshape.12.taps_ref, s32[256,1]{1,0:T(8,128)S(1)} %copy.9.order_ref), custom_call_target="tpu_custom_call" | custom-call | tf_op jit(solution)/shard_map/pallas_call | solution.py:294
  28.9 0.0 copy-start.1
  28.9 1.2 %copy-done.1 = bf16[8,256,256]{2,1,0:T(8,128)(2,1)S(1)} copy-done((bf16[8,256,256]{2,1,0:T(8,128)(2,1)S(1)}, bf16[8,256,256]{2,1,0:T(8,128)(2,1)}, u32[]{:S(2)}) %copy-start.1) | copy-done | bytes 1048600
  30.2 0.0 copy-start.3
  30.2 0.8 %copy-done.3 = bf16[256,128]{1,0:T(8,128)(2,1)S(1)} copy-done((bf16[256,128]{1,0:T(8,128)(2,1)S(1)}, bf16[256,128]{1,0:T(8,128)(2,1)}, u32[]{:S(2)}) %copy-start.3) | copy-done | bytes 65560
  31.0 0.0 copy-start.4
  31.0 0.7 copy-done.4
  31.7 43.7 %shard_map.83 = f32[4,256,256]{2,1,0:T(8,128)} custom-call(s32[16]{0:T(128)S(1)} %copy-done.4, s32[5]{0:T(128)S(1)} %pad_add_fusion.groups_ref, bf16[32,256,128]{2,1,0:T(8,128)(2,1)S(1)} %bitcast.4, bf16[8,2048,256]{2,1,0:T(8,128)(2,1)} %constant.16.clone.dft_ref, bf16[8,256,256]{2,1,0:T(8,128)(2,1)S(1)} %copy-done.1, bf16[256,128]{1,0:T(8,128)(2,1)S(1)} %copy-done.3), custom_call_target="tpu_custom_call" | custom-call | tf_op jit(solution)/shard_map/pallas_call | solution.py:278
  (1 shorter events, 0.0 us)
Async XLA Ops:
  0.0 0.7 copy-start
  2.6 1.0 %copy-start.2 = (bf16[256,1024]{1,0:T(8,128)(2,1)S(1)}, bf16[256,1024]{1,0:T(8,128)(2,1)}, u32[]{:S(2)}) copy-start(bf16[256,1024]{1,0:T(8,128)(2,1)} %raw_ref.1) | copy-start | bytes 1572868
  28.9 1.2 %copy-start.1 = (bf16[8,256,256]{2,1,0:T(8,128)(2,1)S(1)}, bf16[8,256,256]{2,1,0:T(8,128)(2,1)}, u32[]{:S(2)}) copy-start(bf16[8,256,256]{2,1,0:T(8,128)(2,1)} %constant.17.clone.lag_ref) | copy-start | bytes 3145732
  30.2 0.8 %copy-start.3 = (bf16[256,128]{1,0:T(8,128)(2,1)S(1)}, bf16[256,128]{1,0:T(8,128)(2,1)}, u32[]{:S(2)}) copy-start(bf16[256,128]{1,0:T(8,128)(2,1)} %constant.18.clone.ones_ref) | copy-start | bytes 196612
  31.0 0.7 copy-start.4
where the time goes:
time: 75.7 us; the launch traced here: 75.4 us
  Pallas kernels  69 us (91%)
  local copies, waits for them, and re-layouts  6.26 us (8%)
    pallas_call x1, Pallas kernels, correlate(): pl.pallas_call(correlate_kernel, grid_spec=grid_spec, out_shape=jax.Shape...  43.7 us
    pallas_call x1, Pallas kernels, body(): pl.pallas_call(functools.partial(gather_kernel, members), out_shape=jax.S...  25.3 us
    unnamed x10, local copies, waits for them, and re-layouts  4.44 us

commit v1 on v0

v1 whole, which is shorter than its diff:
```python
import functools
import math

import jax
import jax.numpy as jnp
import ml_dtypes
import numpy as np
from jax import lax
from jax.experimental import pallas as pl
from jax.experimental.pallas import tpu as pltpu
from jax.sharding import PartitionSpec as P

SB = 16
DEC = 4
TAPS = 256
SEG = 2048
BAND = 64
LAGS = 256
ROUNDS = 4
BINS = 1024
LANE = 128
SPAN = LANE * DEC + TAPS
GROUPS = ROUNDS + 1
ROWS = GROUPS * SB
THEIRS = ROUNDS * SB
FOLD = SEG // 2
FT = 256
TILES = BINS // FT
PACK = 8
NT = (((1,), (1,)), ((), ()))
QUAD = 4
MESH = pl.DeviceIdType.MESH


def dft_table():
    sample = np.arange(FOLD)
    frequency = np.arange(BINS)
    angles = (sample[None, :] * frequency[:, None] % SEG) * (2.0 * math.pi / SEG)
    taper = (0.5 - 0.5 * np.cos(sample * (2.0 * math.pi / SEG)))[None, :]
    both = np.stack([np.cos(angles) * taper, -np.sin(angles) * taper])
    both[0, :, 0] = 1.0 - 2.0 * (frequency % 2)
    return both.astype(np.float32).astype(ml_dtypes.bfloat16)


def lag_table(window_count):
    frequency = np.arange(BINS)
    offset = np.arange(LAGS) - LAGS // 2 + SEG
    angles = (frequency[None, :] * offset[:, None] % SEG) * (2.0 * math.pi / SEG)
    scale = 1.0 / math.sqrt(BINS * window_count)
    both = np.stack([np.cos(angles) * scale, -np.sin(angles) * scale])
    return both.astype(np.float32).astype(ml_dtypes.bfloat16)


def gather_kernel(members, raw_ref, taps_ref, order_ref, out_ref, halo, low, halo_sems, own_sem, send_sems, recv_sems):
    me = lax.axis_index("sta")
    stations, local_time = raw_ref.shape
    line = members // QUAD
    rank, lead = me // QUAD, me % QUAD
    far = [lax.rem(rank + k, line) * QUAD + lead for k in range(1, line)]
    across = rank * QUAD + lax.rem(lead + 2, QUAD)
    twin = me + 1 - 2 * lax.rem(me, 2)
    after, before = lax.rem(me + 1, members), lax.rem(me + members - 1, members)

    barrier = pltpu.get_barrier_semaphore()
    greeted = far + [across, twin, after, before]
    for peer in greeted:
        pl.semaphore_signal(barrier, inc=1, device_id={"sta": peer}, device_id_type=MESH)
    pl.semaphore_wait(barrier, len(greeted))

    halo_copy = pltpu.make_async_remote_copy(
        src_ref=raw_ref.at[:, local_time - TAPS :],
        dst_ref=halo,
        send_sem=halo_sems.at[0],
        recv_sem=halo_sems.at[1],
        device_id={"sta": after},
        device_id_type=MESH,
    )

    @pl.when(me < members - 1)
    def _():
        halo_copy.start()

    banded = jnp.broadcast_to(taps_ref[...], (LANE, SPAN))
    banded = pltpu.roll(banded, 0, 1, stride=DEC, stride_axis=0).astype(jnp.bfloat16)
    picks = (lax.broadcasted_iota(jnp.int32, (stations, stations), 1) == order_ref[...]).astype(
        jnp.float32
    ).astype(jnp.bfloat16)
    dims = (((1,), (1,)), ((), ()))

    def filtered(piece, samples):
        summed = lax.dot_general(samples, banded, dims, preferred_element_type=jnp.float32)
        ordered = jnp.dot(picks, summed.astype(jnp.bfloat16), preferred_element_type=jnp.float32)
        low[piece] = ordered.astype(jnp.bfloat16)

    for piece in range(1, low.shape[0]):
        first = piece * LANE * DEC - TAPS
        filtered(piece, raw_ref[:, first : first + SPAN])

    @pl.when(me > 0)
    def _():
        halo_copy.wait_recv()

    @pl.when(me == 0)
    def _():
        halo[...] = jnp.zeros_like(halo)

    filtered(0, jnp.concatenate([halo[...], raw_ref[:, : LANE * DEC]], axis=1))

    sent = []

    def send(source, slot, peer):
        n = len(sent)
        copy = pltpu.make_async_remote_copy(
            src_ref=source,
            dst_ref=out_ref.at[slot],
            send_sem=send_sems.at[n],
            recv_sem=recv_sems.at[slot],
            device_id={"sta": peer},
            device_id_type=MESH,
        )
        copy.start()
        sent.append(copy)

    def arrived(slot):
        pltpu.make_async_remote_copy(
            src_ref=low,
            dst_ref=out_ref.at[slot],
            send_sem=send_sems.at[0],
            recv_sem=recv_sems.at[slot],
            device_id={"sta": twin},
            device_id_type=MESH,
        ).wait_recv()

    order = sorted(range(line - 1), key=lambda k: min(k + 1, line - 1 - k))
    for k in order:
        send(low, me, far[k])
    send(low, me, across)
    send(low, me, twin)
    own = pltpu.make_async_copy(low, out_ref.at[me], own_sem)
    own.start()
    shift = across - me
    arrived(me + shift)
    send(out_ref.at[me + shift], me + shift, twin)
    for k in order:
        arrived(far[k])
        send(out_ref.at[far[k]], far[k], across)
        send(out_ref.at[far[k]], far[k], twin)
    for k in order:
        arrived(far[k] + shift)
        send(out_ref.at[far[k] + shift], far[k] + shift, twin)
    turn = twin - me
    for slot in [me] + [far[k] for k in order]:
        arrived(slot + turn)
        arrived(slot + shift + turn)
    own.wait()
    for copy in sent:
        copy.wait_send()

    @pl.when(me < members - 1)
    def _():
        halo_copy.wait_send()


def correlate_kernel(
    starts_ref,
    groups_ref,
    low_ref,
    dft_ref,
    lag_ref,
    out_ref,
    rows,
    ahead,
    back,
    even_theirs,
    odd_theirs,
    even_own,
    odd_own,
    real_theirs,
    imag_theirs,
    white_own,
    left,
    right,
    cross_real,
    cross_imag,
    sems,
):
    tile = pl.program_id(0)
    planes = low_ref.shape[0]
    window_count = starts_ref.shape[0]
    lane = lax.broadcasted_iota(jnp.int32, (1, LANE), 1)

    @pl.when(tile == 0)
    def _():
        copies = []
        for g in range(GROUPS):
            first = pl.multiple_of(groups_ref[g] * SB, SB)
            copy = pltpu.make_async_copy(
                low_ref.at[:, pl.ds(first, SB), :], rows.at[:, pl.ds(g * SB, SB), :], sems.at[g]
            )
            copy.start()
            copies.append(copy)
        for copy in copies:
            copy.wait()
        mirror = (
            lax.broadcasted_iota(jnp.int32, (LANE, LANE), 0) + lax.broadcasted_iota(jnp.int32, (LANE, LANE), 1)
            == LANE - 1
        ).astype(jnp.float32).astype(jnp.bfloat16)
        back[0] = jnp.zeros((ROWS, LANE), jnp.float32)

        def one_plane(n, carry):
            samples = rows[n]
            ahead[n] = samples.astype(jnp.float32)
            back[planes - n] = jnp.dot(samples, mirror, preferred_element_type=jnp.float32)
            return carry

        lax.fori_loop(0, planes, one_plane, 0, unroll=4)

        def one_window(w, carry):
            def shifted(ref, first):
                plane = first // LANE
                keep = LANE - first % LANE
                shift = keep % LANE
                now = pltpu.roll(ref[plane], shift, 1)
                pieces = []
                for piece in range(FOLD // LANE):
                    later = pltpu.roll(ref[plane + piece + 1], shift, 1)
                    pieces.append(jnp.where(lane < keep, now, later))
                    now = later
                return pieces, now

            start = starts_ref[w]
            forward, middle = shifted(ahead, start)
            backward, _ = shifted(back, planes * LANE - 1 - FOLD * 2 + LANE - start)
            theirs = pl.ds(pl.multiple_of(w * THEIRS, SB), THEIRS)
            own = pl.ds(pl.multiple_of(w * SB, SB), SB)
            for piece, (a, b) in enumerate(zip(forward, backward)):
                at = slice(piece * LANE, (piece + 1) * LANE)
                even, odd = a + b, a - b
                if piece == 0:
                    even = jnp.where(lane == 0, middle, even)
                even, odd = even.astype(jnp.bfloat16), odd.astype(jnp.bfloat16)
                even_theirs[theirs, at] = even[:THEIRS]
                odd_theirs[theirs, at] = odd[:THEIRS]
                even_own[own, at] = even[THEIRS:]
                odd_own[own, at] = odd[THEIRS:]
            return carry

        lax.fori_loop(0, window_count, one_window, 0)

    def dot_nt(a, b):
        return lax.dot_general(a, b, NT, preferred_element_type=jnp.float32)

    half = LANE // 2
    pairs = window_count // 2
    real_theirs[...] = dot_nt(dft_ref[0], even_theirs[...])
    imag_theirs[...] = dot_nt(dft_ref[1], odd_theirs[...])

    def one_band(n, carry):
        at = pl.ds(pl.multiple_of(n * BAND, BAND), BAND)
        for pair in range(pairs):
            lanes = slice(pair * LANE, (pair + 1) * LANE)
            real, imag = real_theirs[at, lanes], imag_theirs[at, lanes]
            level = jnp.sum(real * real + imag * imag, axis=0, keepdims=True)
            scale = lax.rsqrt(level * (1.0 / (2 * BAND)) + 1e-06)
            real, imag = real * scale, imag * scale
            real_turned, imag_turned = pltpu.roll(real, half, 1), pltpu.roll(imag, half, 1)
            first = lane < half
            blocks = (
                (jnp.where(first, real, -imag_turned), jnp.where(first, real_turned, -imag)),
                (jnp.where(first, imag, real_turned), jnp.where(first, imag_turned, real)),
            )
            for c, block in enumerate(blocks):
                both = [x.reshape(BAND // PACK, 1, PACK, LANE) for x in block]
                both = jnp.concatenate(both, axis=1).reshape(BAND // PACK, 2 * PACK, LANE)
                right[
                    pl.ds(n * (BAND // PACK), BAND // PACK),
                    pl.ds((c * pairs + pair) * 2 * PACK, 2 * PACK),
                    :,
                ] = both.astype(jnp.bfloat16)
        return carry

    lax.fori_loop(0, FT // BAND, one_band, 0)

    real, imag = dot_nt(even_own[...], dft_ref[0]), dot_nt(odd_own[...], dft_ref[1])
    power = (real * real + imag * imag).astype(jnp.bfloat16)
    same = (
        lax.broadcasted_iota(jnp.int32, (FT, FT), 0) // BAND == lax.broadcasted_iota(jnp.int32, (FT, FT), 1) // BAND
    ).astype(jnp.float32).astype(jnp.bfloat16)
    level = jnp.dot(power, same, preferred_element_type=jnp.float32)
    scale = lax.rsqrt(level * (1.0 / (2 * BAND)) + 1e-06)
    white_own[0] = real * scale
    white_own[1] = imag * scale

    slots = LANE // PACK
    for part in range(FT // LANE):
        for c in range(2):
            moved = [[], []]
            for pair in range(pairs):
                x = [
                    white_own[c, (2 * pair + k) * SB : (2 * pair + k + 1) * SB, part * LANE : (part + 1) * LANE]
                    for k in range(2)
                ]
                low_slot = lane // PACK % 2 == 0
                y = (
                    jnp.where(low_slot, x[0], pltpu.roll(x[1], PACK, 1)),
                    jnp.where(low_slot, pltpu.roll(x[0], LANE - PACK, 1), x[1]),
                )
                for k in range(2):
                    moved[k].append(pltpu.roll(y[k], 2 * PACK * pair, 1) if pair else y[k])
            for slot in range(slots):
                turn, k = slot // 2, slot % 2
                joined = moved[k][0]
                for pair in range(1, pairs):
                    joined = jnp.where(lane // (2 * PACK) == (turn + pair) % (slots // 2), moved[k][pair], joined)
                if turn:
                    joined = pltpu.roll(joined, LANE - 2 * PACK * turn, 1)
                left[part * slots + slot, c] = joined.astype(jnp.bfloat16)

    own_bin = lax.broadcasted_iota(jnp.int32, (PACK * SB, LANE), 0) // SB
    mask = (own_bin == lax.broadcasted_iota(jnp.int32, (PACK * SB, LANE), 1) % PACK).astype(jnp.float32).astype(
        jnp.bfloat16
    )

    def one_group(n, carry):
        masked = jnp.concatenate([jnp.concatenate([left[n, c]] * PACK, axis=0) * mask for c in range(2)], axis=1)
        product = jnp.dot(masked, right[n], preferred_element_type=jnp.float32)
        product = product.reshape(PACK, 2, SB // 2, LANE)
        first = lane < half
        a, b = product[:, 0].reshape(PACK * SB // 2, LANE), product[:, 1].reshape(PACK * SB // 2, LANE)
        a_turned, b_turned = pltpu.roll(a, half, 1), pltpu.roll(b, half, 1)
        at = pl.ds(pl.multiple_of((tile * (FT // PACK) + n) * PACK * SB // 2, PACK * SB // 2), PACK * SB // 2)
        cross_real[at, :] = jnp.where(first, a, b_turned)
        cross_imag[at, :] = jnp.where(first, a_turned, b)
        return carry

    lax.fori_loop(0, FT // PACK, one_group, 0, unroll=4)

    @pl.when(tile == pl.num_programs(0) - 1)
    def _():
        def two_stations(n, carry):
            summed = None
            for k, cross in enumerate((cross_real, cross_imag)):
                columns = jnp.concatenate(
                    [cross[pl.ds(2 * n + m, BINS, stride=SB // 2), :].astype(jnp.bfloat16) for m in range(2)], axis=1
                )
                term = jnp.dot(lag_ref[k], columns, preferred_element_type=jnp.float32)
                summed = term if summed is None else summed + term
            turned = summed.T
            for m in range(2):
                for h in range(2):
                    i = h * (SB // 2) + 2 * n + m
                    for r in range(ROUNDS):
                        first = ((m * 2 + h) * ROUNDS + r) * SB
                        out_ref[r, pl.ds(pl.multiple_of(i * SB, SB), SB), :] = turned[first : first + SB]
            return carry

        lax.fori_loop(0, SB // 4, two_stations, 0)


def correlate(window_starts, groups, low, dft, lag):
    window_count = window_starts.shape[0]
    planes = low.shape[0]
    grid_spec = pltpu.PrefetchScalarGridSpec(
        num_scalar_prefetch=2,
        grid=(TILES,),
        in_specs=[
            pl.BlockSpec(memory_space=pl.ANY),
            pl.BlockSpec((2, FT, FOLD), lambda n, *_: (0, n, 0)),
            pl.BlockSpec((2, LAGS, BINS), lambda n, *_: (0, 0, 0)),
        ],
        out_specs=pl.BlockSpec((ROUNDS, SB * SB, LAGS), lambda n, *_: (0, 0, 0)),
        scratch_shapes=[
            pltpu.VMEM((planes, ROWS, LANE), jnp.bfloat16),
            pltpu.VMEM((planes, ROWS, LANE), jnp.float32),
            pltpu.VMEM((planes + 1, ROWS, LANE), jnp.float32),
            pltpu.VMEM((window_count * THEIRS, FOLD), jnp.bfloat16),
            pltpu.VMEM((window_count * THEIRS, FOLD), jnp.bfloat16),
            pltpu.VMEM((window_count * SB, FOLD), jnp.bfloat16),
            pltpu.VMEM((window_count * SB, FOLD), jnp.bfloat16),
            pltpu.VMEM((FT, window_count * THEIRS), jnp.float32),
            pltpu.VMEM((FT, window_count * THEIRS), jnp.float32),
            pltpu.VMEM((2, window_count * SB, FT), jnp.float32),
            pltpu.VMEM((FT // PACK, 2, SB, LANE), jnp.bfloat16),
            pltpu.VMEM((FT // PACK, 2 * LANE, LANE), jnp.bfloat16),
            pltpu.VMEM((BINS * SB // 2, LANE), jnp.float32),
            pltpu.VMEM((BINS * SB // 2, LANE), jnp.float32),
            pltpu.SemaphoreType.DMA((GROUPS,)),
        ],
    )
    return pl.pallas_call(
        correlate_kernel,
        grid_spec=grid_spec,
        out_shape=jax.ShapeDtypeStruct((ROUNDS, SB * SB, LAGS), jnp.float32),
        compiler_params=pltpu.CompilerParams(vmem_limit_bytes=56 * 2**20),
    )(window_starts, groups, low, dft, lag)


def body(raw_traces, filter_taps, station_order, window_starts, pairing):
    members = lax.axis_size("sta")
    me = lax.axis_index("sta")
    stations, local_time = raw_traces.shape
    window_count = window_starts.shape[0]
    pieces = local_time // (LANE * DEC)
    taps = jnp.pad(filter_taps.astype(jnp.float32)[::-1], (DEC, SPAN - TAPS - DEC)).reshape(1, SPAN)
    in_vmem = pl.BlockSpec(memory_space=pltpu.VMEM)
    low = pl.pallas_call(
        functools.partial(gather_kernel, members),
        out_shape=jax.ShapeDtypeStruct((members, pieces, stations, LANE), jnp.bfloat16),
        in_specs=[in_vmem] * 3,
        out_specs=pl.BlockSpec(memory_space=pl.ANY),
        scratch_shapes=[
            pltpu.VMEM((stations, TAPS), jnp.bfloat16),
            pltpu.VMEM((pieces, stations, LANE), jnp.bfloat16),
            pltpu.SemaphoreType.DMA((2,)),
            pltpu.SemaphoreType.DMA,
            pltpu.SemaphoreType.DMA((members,)),
            pltpu.SemaphoreType.DMA((members,)),
        ],
        compiler_params=pltpu.CompilerParams(
            collective_id=0, has_side_effects=True, vmem_limit_bytes=40 * 2**20
        ),
    )(raw_traces, taps, station_order.reshape(stations, 1))
    low = low.reshape(members * pieces, stations, LANE)
    groups = jnp.concatenate([lax.dynamic_slice_in_dim(pairing, me, 1, 1)[:, 0], me[None].astype(jnp.int32)])
    correlated = correlate(
        window_starts,
        groups,
        low,
        jnp.asarray(dft_table()),
        jnp.asarray(lag_table(window_count)),
    )
    return correlated.reshape(ROUNDS, SB, SB, LAGS)


def solution(mesh):
    return jax.shard_map(
        body,
        mesh=mesh,
        in_specs=(P("parts", "sta"), P(), P("parts"), P("parts"), P()),
        out_specs=P(None, ("parts", "sta"), None, None),
        check_vma=False,
    )
```

time: 75.7 us -> 65.6 us (0.87)
  Pallas kernels: 69 us -> 59.8 us
  local copies, waits for them, and re-layouts: 6.26 us -> 4.88 us
    pallas_call x1, Pallas kernels: 43.7 us -> 34.5 us  [correlate(): pl.pallas_call(correlate_kernel, grid_spec=grid_spec, out_shape=jax.Shape...]
    unnamed x10 -> x6, local copies, waits for them, and re-layouts: 4.44 us -> 3.06 us
where the time goes in v1:
time: 65.6 us; the launch traced here: 65.4 us
  Pallas kernels  59.8 us (91%)
  local copies, waits for them, and re-layouts  4.88 us (7%)
    pallas_call x1, Pallas kernels, correlate(): pl.pallas_call(correlate_kernel, grid_spec=grid_spec, out_shape=jax.Shape...  34.5 us
    pallas_call x1, Pallas kernels, body(): pl.pallas_call(functools.partial(gather_kernel, members), out_shape=jax.S...  25.3 us
    unnamed x6, local copies, waits for them, and re-layouts  3.06 us

profile of v1, /device:TPU:0, one launch (start us, length us, event | category | flops | bytes accessed | tf_op | source)
XLA Modules:
  0.0 65.4 jit_solution(9166518623758236011)
XLA Ops:
  0.0 0.0 copy-start
  0.0 0.7 %copy-done = s32[4,16]{1,0:T(4,128)S(1)} copy-done((s32[4,16]{1,0:T(4,128)S(1)}, s32[4,16]{1,0:T(4,128)}, u32[]{:S(2)}) %copy-start) | copy-done | bytes 280
  0.7 0.2 dynamic-slice_reduce_fusion
  0.9 0.6 pad_add_fusion.groups_ref
  1.5 0.7 %rev.3 = f32[256]{0:T(256)S(1)} reverse(bf16[256]{0:T(256)(128)(2,1)} %param.8), dimensions={0} | reverse | bytes 1536 | tf_op jit(solution)/shard_map/rev | solution.py:404
  2.2 0.1 pad.4
  2.3 0.8 %copy.8.order_ref = s32[256,1]{1,0:T(8,128)S(1)} copy(s32[256,1]{0,1:T(1,128)} %bitcast.5) | data formatting | bytes 2048 | tf_op jit(solution)/shard_map/reshape | solution.py:422
  3.1 0.0 copy-start.2
  3.1 1.0 %copy-done.2 = bf16[256,1024]{1,0:T(8,128)(2,1)S(1)} copy-done((bf16[256,1024]{1,0:T(8,128)(2,1)S(1)}, bf16[256,1024]{1,0:T(8,128)(2,1)}, u32[]{:S(2)}) %copy-start.2) | copy-done | bytes 524312
  4.2 25.3 %shard_map.73 = bf16[16,2,256,128]{3,2,1,0:T(8,128)(2,1)S(1)} custom-call(bf16[256,1024]{1,0:T(8,128)(2,1)S(1)} %copy-done.2, f32[1,768]{1,0:T(1,128)S(1)} %reshape.12.taps_ref, s32[256,1]{1,0:T(8,128)S(1)} %copy.8.order_ref), custom_call_target="tpu_custom_call" | custom-call | tf_op jit(solution)/shard_map/pallas_call | solution.py:406
  29.5 0.0 copy-start.1
  29.5 1.3 %copy-done.1 = bf16[16,2,256,128]{3,2,1,0:T(8,128)(2,1)} copy-done((bf16[16,2,256,128]{3,2,1,0:T(8,128)(2,1)}, bf16[16,2,256,128]{3,2,1,0:T(8,128)(2,1)S(1)}, u32[]{:S(2)}) %copy-start.1) | copy-done | bytes 2097176
  30.8 34.5 %shard_map.74 = f32[4,256,256]{2,1,0:T(8,128)} custom-call(s32[16]{0:T(128)} %starts_ref.1, s32[5]{0:T(128)} %pad_add_fusion.groups_ref, bf16[32,256,128]{2,1,0:T(8,128)(2,1)} %bitcast.4, bf16[2,1024,1024]{2,1,0:T(8,128)(2,1)} %constant.14.clone.dft_ref, bf16[2,256,1024]{2,1,0:T(8,128)(2,1)} %constant.15.clone.lag_ref), custom_call_target="tpu_custom_call" | custom-call | tf_op jit(solution)/shard_map/pallas_call | solution.py:390
  (1 shorter events, 0.0 us)
Async XLA Ops:
  0.0 0.7 %copy-start = (s32[4,16]{1,0:T(4,128)S(1)}, s32[4,16]{1,0:T(4,128)}, u32[]{:S(2)}) copy-start(s32[4,16]{1,0:T(4,128)} %param.11) | copy-start | bytes 772
  3.1 1.0 %copy-start.2 = (bf16[256,1024]{1,0:T(8,128)(2,1)S(1)}, bf16[256,1024]{1,0:T(8,128)(2,1)}, u32[]{:S(2)}) copy-start(bf16[256,1024]{1,0:T(8,128)(2,1)} %raw_ref.1) | copy-start | bytes 1572868
  29.5 1.3 %copy-start.1 = (bf16[16,2,256,128]{3,2,1,0:T(8,128)(2,1)}, bf16[16,2,256,128]{3,2,1,0:T(8,128)(2,1)S(1)}, u32[]{:S(2)}) copy-start(bf16[16,2,256,128]{3,2,1,0:T(8,128)(2,1)S(1)} %shard_map.73) | copy-start | bytes 6291460

commit v2 on v1

--- a/solution.py
+++ b/solution.py
@@ -175,8 +175,6 @@
     odd_theirs,
     even_own,
     odd_own,
-    real_theirs,
-    imag_theirs,
     white_own,
     left,
     right,
@@ -213,7 +211,7 @@
             back[planes - n] = jnp.dot(samples, mirror, preferred_element_type=jnp.float32)
             return carry
 
-        lax.fori_loop(0, planes, one_plane, 0, unroll=4)
+        lax.fori_loop(0, planes, one_plane, 0, unroll=8)
 
         def one_window(w, carry):
             def shifted(ref, first):
@@ -245,41 +243,40 @@
                 odd_own[own, at] = odd[THEIRS:]
             return carry
 
-        lax.fori_loop(0, window_count, one_window, 0)
+        lax.fori_loop(0, window_count, one_window, 0, unroll=2)
 
     def dot_nt(a, b):
         return lax.dot_general(a, b, NT, preferred_element_type=jnp.float32)
 
     half = LANE // 2
     pairs = window_count // 2
-    real_theirs[...] = dot_nt(dft_ref[0], even_theirs[...])
-    imag_theirs[...] = dot_nt(dft_ref[1], odd_theirs[...])
-
-    def one_band(n, carry):
-        at = pl.ds(pl.multiple_of(n * BAND, BAND), BAND)
-        for pair in range(pairs):
-            lanes = slice(pair * LANE, (pair + 1) * LANE)
-            real, imag = real_theirs[at, lanes], imag_theirs[at, lanes]
-            level = jnp.sum(real * real + imag * imag, axis=0, keepdims=True)
-            scale = lax.rsqrt(level * (1.0 / (2 * BAND)) + 1e-06)
-            real, imag = real * scale, imag * scale
-            real_turned, imag_turned = pltpu.roll(real, half, 1), pltpu.roll(imag, half, 1)
-            first = lane < half
-            blocks = (
-                (jnp.where(first, real, -imag_turned), jnp.where(first, real_turned, -imag)),
-                (jnp.where(first, imag, real_turned), jnp.where(first, imag_turned, real)),
-            )
-            for c, block in enumerate(blocks):
-                both = [x.reshape(BAND // PACK, 1, PACK, LANE) for x in block]
-                both = jnp.concatenate(both, axis=1).reshape(BAND // PACK, 2 * PACK, LANE)
-                right[
-                    pl.ds(n * (BAND // PACK), BAND // PACK),
-                    pl.ds((c * pairs + pair) * 2 * PACK, 2 * PACK),
-                    :,
-                ] = both.astype(jnp.bfloat16)
-        return carry
-
-    lax.fori_loop(0, FT // BAND, one_band, 0)
+    wide = 2 * LANE
+    first = lane < half
+    for tile_pair in range(window_count * THEIRS // wide):
+        at = slice(tile_pair * wide, (tile_pair + 1) * wide)
+        reals = dot_nt(dft_ref[0], even_theirs[at, :])
+        imags = dot_nt(dft_ref[1], odd_theirs[at, :])
+        for n in range(FT // BAND):
+            for inner in range(wide // LANE):
+                pair = tile_pair * (wide // LANE) + inner
+                real, imag = (
+                    x[n * BAND : (n + 1) * BAND, inner * LANE : (inner + 1) * LANE] for x in (reals, imags)
+                )
+                level = jnp.sum(real * real + imag * imag, axis=0, keepdims=True)
+                scale = lax.rsqrt(level * (1.0 / (2 * BAND)) + 1e-06)
+                real, imag = real * scale, imag * scale
+                real_turned, imag_turned = pltpu.roll(real, half, 1), pltpu.roll(imag, half, 1)
+                blocks = (
+                    (jnp.where(first, real, -imag_turned), jnp.where(first, real_turned, -imag)),
+                    (jnp.where(first, imag, real_turned), jnp.where(first, imag_turned, real)),
+                )
+                for c, block in enumerate(blocks):
+                    both = [x.reshape(BAND // PACK, 1, PACK, LANE) for x in block]
+                    both = jnp.concatenate(both, axis=1).reshape(BAND // PACK, 2 * PACK, LANE)
+                    row = (c * pairs + pair) * 2 * PACK
+                    right[n * (BAND // PACK) : (n + 1) * (BAND // PACK), row : row + 2 * PACK, :] = both.astype(
+                        jnp.bfloat16
+                    )
 
     real, imag = dot_nt(even_own[...], dft_ref[0]), dot_nt(odd_own[...], dft_ref[1])
     power = (real * real + imag * imag).astype(jnp.bfloat16)
@@ -333,7 +330,7 @@
         cross_imag[at, :] = jnp.where(first, a_turned, b)
         return carry
 
-    lax.fori_loop(0, FT // PACK, one_group, 0, unroll=4)
+    lax.fori_loop(0, FT // PACK, one_group, 0, unroll=16)
 
     @pl.when(tile == pl.num_programs(0) - 1)
     def _():
@@ -354,7 +351,7 @@
                         out_ref[r, pl.ds(pl.multiple_of(i * SB, SB), SB), :] = turned[first : first + SB]
             return carry
 
-        lax.fori_loop(0, SB // 4, two_stations, 0)
+        lax.fori_loop(0, SB // 4, two_stations, 0, unroll=True)
 
 
 def correlate(window_starts, groups, low, dft, lag):
@@ -377,8 +374,6 @@
             pltpu.VMEM((window_count * THEIRS, FOLD), jnp.bfloat16),
             pltpu.VMEM((window_count * SB, FOLD), jnp.bfloat16),
             pltpu.VMEM((window_count * SB, FOLD), jnp.bfloat16),
-            pltpu.VMEM((FT, window_count * THEIRS), jnp.float32),
-            pltpu.VMEM((FT, window_count * THEIRS), jnp.float32),
             pltpu.VMEM((2, window_count * SB, FT), jnp.float32),
             pltpu.VMEM((FT // PACK, 2, SB, LANE), jnp.bfloat16),
             pltpu.VMEM((FT // PACK, 2 * LANE, LANE), jnp.bfloat16),

time: 65.6 us -> 54.4 us (0.83)
  Pallas kernels: 59.8 us -> 48.6 us
    pallas_call x1, Pallas kernels: 34.5 us -> 23.3 us  [correlate(): pl.pallas_call(correlate_kernel, grid_spec=grid_spec, out_shape=jax.Shape...]
where the time goes in v2:
time: 54.4 us; the launch traced here: 54.1 us
  Pallas kernels  48.6 us (89%)
  local copies, waits for them, and re-layouts  4.88 us (9%)
  other arithmetic  0.62 us (1%)
    pallas_call x1, Pallas kernels, body(): pl.pallas_call(functools.partial(gather_kernel, members), out_shape=jax.S...  25.3 us
    pallas_call x1, Pallas kernels, correlate(): pl.pallas_call(correlate_kernel, grid_spec=grid_spec, out_shape=jax.Shape...  23.3 us
    unnamed x6, local copies, waits for them, and re-layouts  3.06 us

profile of v2, /device:TPU:0, one launch (start us, length us, event | category | flops | bytes accessed | tf_op | source)
XLA Modules:
  0.0 54.1 jit_solution(3218999238110787877)
XLA Ops:
  0.0 0.0 copy-start
  0.0 0.7 %copy-done = s32[4,16]{1,0:T(4,128)S(1)} copy-done((s32[4,16]{1,0:T(4,128)S(1)}, s32[4,16]{1,0:T(4,128)}, u32[]{:S(2)}) %copy-start) | copy-done | bytes 280
  0.7 0.2 dynamic-slice_reduce_fusion
  0.9 0.6 %pad_add_fusion.groups_ref = s32[5]{0:T(128)} fusion(s32[1]{0:T(128)} %bitcast, s32[4]{0:T(128)S(1)} %dynamic-slice_reduce_fusion), kind=kLoop, calls=%fused_computation.1 | loop fusion | flops 5 | bytes 40 | tf_op jit(solution)/shard_map/concatenate | solution.py:419
  1.5 0.7 %rev.3 = f32[256]{0:T(256)S(1)} reverse(bf16[256]{0:T(256)(128)(2,1)} %param.8), dimensions={0} | reverse | bytes 1536 | tf_op jit(solution)/shard_map/rev | solution.py:399
  2.2 0.1 pad.4
  2.3 0.8 %copy.8.order_ref = s32[256,1]{1,0:T(8,128)S(1)} copy(s32[256,1]{0,1:T(1,128)} %bitcast.5) | data formatting | bytes 2048 | tf_op jit(solution)/shard_map/reshape | solution.py:417
  3.1 0.0 copy-start.2
  3.1 1.0 %copy-done.2 = bf16[256,1024]{1,0:T(8,128)(2,1)S(1)} copy-done((bf16[256,1024]{1,0:T(8,128)(2,1)S(1)}, bf16[256,1024]{1,0:T(8,128)(2,1)}, u32[]{:S(2)}) %copy-start.2) | copy-done | bytes 524312
  4.2 25.3 %shard_map.73 = bf16[16,2,256,128]{3,2,1,0:T(8,128)(2,1)S(1)} custom-call(bf16[256,1024]{1,0:T(8,128)(2,1)S(1)} %copy-done.2, f32[1,768]{1,0:T(1,128)S(1)} %reshape.12.taps_ref, s32[256,1]{1,0:T(8,128)S(1)} %copy.8.order_ref), custom_call_target="tpu_custom_call" | custom-call | tf_op jit(solution)/shard_map/pallas_call | solution.py:401
  29.5 0.0 copy-start.1
  29.5 1.3 %copy-done.1 = bf16[16,2,256,128]{3,2,1,0:T(8,128)(2,1)} copy-done((bf16[16,2,256,128]{3,2,1,0:T(8,128)(2,1)}, bf16[16,2,256,128]{3,2,1,0:T(8,128)(2,1)S(1)}, u32[]{:S(2)}) %copy-start.1) | copy-done | bytes 2097176
  30.8 23.3 %shard_map.74 = f32[4,256,256]{2,1,0:T(8,128)} custom-call(s32[16]{0:T(128)} %starts_ref.1, s32[5]{0:T(128)} %pad_add_fusion.groups_ref, bf16[32,256,128]{2,1,0:T(8,128)(2,1)} %bitcast.4, bf16[2,1024,1024]{2,1,0:T(8,128)(2,1)} %constant.14.clone.dft_ref, bf16[2,256,1024]{2,1,0:T(8,128)(2,1)} %constant.15.clone.lag_ref), custom_call_target="tpu_custom_call" | custom-call | tf_op jit(solution)/shard_map/pallas_call | solution.py:385
  (1 shorter events, 0.0 us)
Async XLA Ops:
  0.0 0.7 %copy-start = (s32[4,16]{1,0:T(4,128)S(1)}, s32[4,16]{1,0:T(4,128)}, u32[]{:S(2)}) copy-start(s32[4,16]{1,0:T(4,128)} %param.11) | copy-start | bytes 772
  3.1 1.0 %copy-start.2 = (bf16[256,1024]{1,0:T(8,128)(2,1)S(1)}, bf16[256,1024]{1,0:T(8,128)(2,1)}, u32[]{:S(2)}) copy-start(bf16[256,1024]{1,0:T(8,128)(2,1)} %raw_ref.1) | copy-start | bytes 1572868
  29.5 1.3 %copy-start.1 = (bf16[16,2,256,128]{3,2,1,0:T(8,128)(2,1)}, bf16[16,2,256,128]{3,2,1,0:T(8,128)(2,1)S(1)}, u32[]{:S(2)}) copy-start(bf16[16,2,256,128]{3,2,1,0:T(8,128)(2,1)S(1)} %shard_map.73) | copy-start | bytes 6291460

commit v3 on v2

--- a/solution.py
+++ b/solution.py
@@ -51,20 +51,63 @@
     return both.astype(np.float32).astype(ml_dtypes.bfloat16)
 
 
-def gather_kernel(members, raw_ref, taps_ref, order_ref, out_ref, halo, low, halo_sems, own_sem, send_sems, recv_sems):
+def gather_kernel(
+    members,
+    raw_ref,
+    taps_ref,
+    order_ref,
+    pairing_ref,
+    out_ref,
+    raw,
+    halo,
+    column,
+    private,
+    picked,
+    raw_sem,
+    halo_sems,
+    line_send,
+    line_recv,
+    pick_send,
+    pick_recv,
+):
     me = lax.axis_index("sta")
     stations, local_time = raw_ref.shape
-    line = members // QUAD
+    line, pieces = column.shape[:2]
     rank, lead = me // QUAD, me % QUAD
-    far = [lax.rem(rank + k, line) * QUAD + lead for k in range(1, line)]
+    turn = 1 - 2 * lax.rem(me, 2)
+    twin = me + turn
     across = rank * QUAD + lax.rem(lead + 2, QUAD)
-    twin = me + 1 - 2 * lax.rem(me, 2)
+    others = (across, across + turn, twin)
     after, before = lax.rem(me + 1, members), lax.rem(me + members - 1, members)
 
+    def nearest(n):
+        chosen = None
+        for r in range(line):
+            order = sorted((x for x in range(line) if x != r), key=lambda x: abs(x - r))
+            chosen = order[n] if chosen is None else jnp.where(rank == r, order[n], chosen)
+        return chosen
+
+    line_order = [nearest(n) for n in range(line - 1)]
+
+    raw_copy = pltpu.make_async_copy(raw_ref, raw, raw_sem)
+    raw_copy.start()
+
     barrier = pltpu.get_barrier_semaphore()
-    greeted = far + [across, twin, after, before]
+    greeted = [r * QUAD + lead for r in line_order] + list(others) + [after, before]
     for peer in greeted:
         pl.semaphore_signal(barrier, inc=1, device_id={"sta": peer}, device_id_type=MESH)
+
+    mirror = (
+        lax.broadcasted_iota(jnp.int32, (TAPS, TAPS), 0) + lax.broadcasted_iota(jnp.int32, (TAPS, TAPS), 1) == TAPS - 1
+    ).astype(jnp.float32).astype(jnp.bfloat16)
+    taps = jnp.broadcast_to(taps_ref[...].astype(jnp.float32), (SB, TAPS)).astype(jnp.bfloat16)
+    taps = jnp.dot(taps, mirror, preferred_element_type=jnp.float32)[:1]
+    banded = jnp.concatenate([taps, jnp.zeros((1, SPAN - TAPS), jnp.float32)], axis=1)
+    banded = jnp.broadcast_to(banded, (LANE, SPAN))
+    banded = pltpu.roll(banded, DEC, 1, stride=DEC, stride_axis=0).astype(jnp.bfloat16)
+    picks = (lax.broadcasted_iota(jnp.int32, (stations, stations), 0) == order_ref[...]).astype(jnp.float32)
+    picks = picks.T.astype(jnp.bfloat16)
+
     pl.semaphore_wait(barrier, len(greeted))
 
     halo_copy = pltpu.make_async_remote_copy(
@@ -80,21 +123,66 @@
     def _():
         halo_copy.start()
 
-    banded = jnp.broadcast_to(taps_ref[...], (LANE, SPAN))
-    banded = pltpu.roll(banded, 0, 1, stride=DEC, stride_axis=0).astype(jnp.bfloat16)
-    picks = (lax.broadcasted_iota(jnp.int32, (stations, stations), 1) == order_ref[...]).astype(
-        jnp.float32
-    ).astype(jnp.bfloat16)
+    def line_copy(source, piece, n, peer):
+        return pltpu.make_async_remote_copy(
+            src_ref=column.at[source, piece],
+            dst_ref=column.at[source, piece],
+            send_sem=line_send.at[piece * line + n],
+            recv_sem=line_recv.at[source * pieces + piece],
+            device_id={"sta": peer * QUAD + lead},
+            device_id_type=MESH,
+        )
+
+    at_end = (rank == 0) | (rank == line - 1)
+    beside_end = (rank == 1) | (rank == line - 2)
+    far_end = jnp.where(rank == 1, 0, line - 1)
+    relayed = line > 3
+    picks_sent = []
+
+    def share(source, piece, samples):
+        private[...] = samples.reshape(private.shape)
+        plane = (source * QUAD + lead) * pieces + piece
+        for k, peer in enumerate(others + (me,)):
+            blocks = [pairing_ref[r, peer] for r in range(ROUNDS)] + [peer]
+            slot = len(picks_sent)
+            for g, block in enumerate(blocks):
+                chosen = private[block]
+                if k < len(others):
+                    picked[slot, g * SB : (g + 1) * SB, :] = chosen
+                else:
+                    out_ref[plane, g * SB : (g + 1) * SB, :] = chosen
+            if k < len(others):
+                copy = pltpu.make_async_remote_copy(
+                    src_ref=picked.at[slot],
+                    dst_ref=out_ref.at[plane],
+                    send_sem=pick_send.at[slot],
+                    recv_sem=pick_recv.at[plane],
+                    device_id={"sta": peer},
+                    device_id_type=MESH,
+                )
+                copy.start()
+                picks_sent.append(copy)
+
     dims = (((1,), (1,)), ((), ()))
 
     def filtered(piece, samples):
         summed = lax.dot_general(samples, banded, dims, preferred_element_type=jnp.float32)
-        ordered = jnp.dot(picks, summed.astype(jnp.bfloat16), preferred_element_type=jnp.float32)
-        low[piece] = ordered.astype(jnp.bfloat16)
-
-    for piece in range(1, low.shape[0]):
+        ordered = jnp.dot(picks, summed.astype(jnp.bfloat16), preferred_element_type=jnp.float32).astype(jnp.bfloat16)
+        column[rank, piece] = ordered
+        for n, peer in enumerate(line_order):
+            if n == line - 2 and relayed:
+
+                @pl.when(jnp.logical_not(at_end))
+                def _():
+                    line_copy(rank, piece, n, peer).start()
+            else:
+                line_copy(rank, piece, n, peer).start()
+        share(rank, piece, ordered)
+
+    raw_copy.wait()
+    for piece in range(pieces - 1, 0, -1):
         first = piece * LANE * DEC - TAPS
-        filtered(piece, raw_ref[:, first : first + SPAN])
+        filtered(piece, raw[:, first : first + SPAN])
 
     @pl.when(me > 0)
     def _():
@@ -104,57 +192,48 @@
     def _():
         halo[...] = jnp.zeros_like(halo)
 
-    filtered(0, jnp.concatenate([halo[...], raw_ref[:, : LANE * DEC]], axis=1))
-
-    sent = []
-
-    def send(source, slot, peer):
-        n = len(sent)
-        copy = pltpu.make_async_remote_copy(
-            src_ref=source,
-            dst_ref=out_ref.at[slot],
-            send_sem=send_sems.at[n],
-            recv_sem=recv_sems.at[slot],
-            device_id={"sta": peer},
-            device_id_type=MESH,
-        )
-        copy.start()
-        sent.append(copy)
-
-    def arrived(slot):
-        pltpu.make_async_remote_copy(
-            src_ref=low,
-            dst_ref=out_ref.at[slot],
-            send_sem=send_sems.at[0],
-            recv_sem=recv_sems.at[slot],
-            device_id={"sta": twin},
-            device_id_type=MESH,
-        ).wait_recv()
-
-    order = sorted(range(line - 1), key=lambda k: min(k + 1, line - 1 - k))
-    for k in order:
-        send(low, me, far[k])
-    send(low, me, across)
-    send(low, me, twin)
-    own = pltpu.make_async_copy(low, out_ref.at[me], own_sem)
-    own.start()
-    shift = across - me
-    arrived(me + shift)
-    send(out_ref.at[me + shift], me + shift, twin)
-    for k in order:
-        arrived(far[k])
-        send(out_ref.at[far[k]], far[k], across)
-        send(out_ref.at[far[k]], far[k], twin)
-    for k in order:
-        arrived(far[k] + shift)
-        send(out_ref.at[far[k] + shift], far[k] + shift, twin)
-    turn = twin - me
-    for slot in [me] + [far[k] for k in order]:
-        arrived(slot + turn)
-        arrived(slot + shift + turn)
-    own.wait()
-    for copy in sent:
+    filtered(0, jnp.concatenate([halo[...], raw[:, : LANE * DEC]], axis=1))
+
+    for n, source in enumerate(line_order):
+        for piece in range(pieces - 1, -1, -1):
+            line_copy(source, piece, n, source).wait_recv()
+            if n == line - 2 and relayed:
+
+                @pl.when(beside_end)
+                def _():
+                    line_copy(source, piece, line - 1, far_end).start()
+
+            share(source, piece, column[source, piece])
+
+    for source in range(line):
+        for piece in range(pieces):
+            for peer in others:
+                plane = peer - rank * QUAD + source * QUAD
+                plane = plane * pieces + piece
+                pltpu.make_async_remote_copy(
+                    src_ref=picked.at[0],
+                    dst_ref=out_ref.at[plane],
+                    send_sem=pick_send.at[0],
+                    recv_sem=pick_recv.at[plane],
+                    device_id={"sta": twin},
+                    device_id_type=MESH,
+                ).wait_recv()
+    for copy in picks_sent:
         copy.wait_send()
+    for piece in range(pieces):
+        for n, peer in enumerate(line_order):
+            if n == line - 2 and relayed:
+
+                @pl.when(jnp.logical_not(at_end))
+                def _():
+                    line_copy(rank, piece, n, peer).wait_send()
+            else:
+                line_copy(rank, piece, n, peer).wait_send()
+        if relayed:
+
+            @pl.when(beside_end)
+            def _():
+                line_copy(line_order[-1], piece, line - 1, far_end).wait_send()
 
     @pl.when(me < members - 1)
     def _():
@@ -163,12 +242,10 @@
 
 def correlate_kernel(
     starts_ref,
-    groups_ref,
     low_ref,
     dft_ref,
     lag_ref,
     out_ref,
-    rows,
     ahead,
     back,
     even_theirs,
@@ -180,7 +257,6 @@
     right,
     cross_real,
     cross_imag,
-    sems,
 ):
     tile = pl.program_id(0)
     planes = low_ref.shape[0]
@@ -189,16 +265,6 @@
 
     @pl.when(tile == 0)
     def _():
-        copies = []
-        for g in range(GROUPS):
-            first = pl.multiple_of(groups_ref[g] * SB, SB)
-            copy = pltpu.make_async_copy(
-                low_ref.at[:, pl.ds(first, SB), :], rows.at[:, pl.ds(g * SB, SB), :], sems.at[g]
-            )
-            copy.start()
-            copies.append(copy)
-        for copy in copies:
-            copy.wait()
         mirror = (
             lax.broadcasted_iota(jnp.int32, (LANE, LANE), 0) + lax.broadcasted_iota(jnp.int32, (LANE, LANE), 1)
             == LANE - 1
@@ -206,7 +272,7 @@
         back[0] = jnp.zeros((ROWS, LANE), jnp.float32)
 
         def one_plane(n, carry):
-            samples = rows[n]
+            samples = low_ref[n]
             ahead[n] = samples.astype(jnp.float32)
             back[planes - n] = jnp.dot(samples, mirror, preferred_element_type=jnp.float32)
             return carry
@@ -354,20 +420,19 @@
         lax.fori_loop(0, SB // 4, two_stations, 0, unroll=True)
 
 
-def correlate(window_starts, groups, low, dft, lag):
+def correlate(window_starts, low, dft, lag):
     window_count = window_starts.shape[0]
     planes = low.shape[0]
     grid_spec = pltpu.PrefetchScalarGridSpec(
-        num_scalar_prefetch=2,
+        num_scalar_prefetch=1,
         grid=(TILES,),
         in_specs=[
-            pl.BlockSpec(memory_space=pl.ANY),
+            pl.BlockSpec((planes, ROWS, LANE), lambda n, *_: (0, 0, 0)),
             pl.BlockSpec((2, FT, FOLD), lambda n, *_: (0, n, 0)),
             pl.BlockSpec((2, LAGS, BINS), lambda n, *_: (0, 0, 0)),
         ],
         out_specs=pl.BlockSpec((ROUNDS, SB * SB, LAGS), lambda n, *_: (0, 0, 0)),
         scratch_shapes=[
-            pltpu.VMEM((planes, ROWS, LANE), jnp.bfloat16),
             pltpu.VMEM((planes, ROWS, LANE), jnp.float32),
             pltpu.VMEM((planes + 1, ROWS, LANE), jnp.float32),
             pltpu.VMEM((window_count * THEIRS, FOLD), jnp.bfloat16),
@@ -379,7 +444,6 @@
             pltpu.VMEM((FT // PACK, 2 * LANE, LANE), jnp.bfloat16),
             pltpu.VMEM((BINS * SB // 2, LANE), jnp.float32),
             pltpu.VMEM((BINS * SB // 2, LANE), jnp.float32),
-            pltpu.SemaphoreType.DMA((GROUPS,)),
         ],
     )
     return pl.pallas_call(
@@ -387,43 +451,44 @@
         grid_spec=grid_spec,
         out_shape=jax.ShapeDtypeStruct((ROUNDS, SB * SB, LAGS), jnp.float32),
         compiler_params=pltpu.CompilerParams(vmem_limit_bytes=56 * 2**20),
-    )(window_starts, groups, low, dft, lag)
+    )(window_starts, low, dft, lag)
 
 
 def body(raw_traces, filter_taps, station_order, window_starts, pairing):
     members = lax.axis_size("sta")
-    me = lax.axis_index("sta")
     stations, local_time = raw_traces.shape
     window_count = window_starts.shape[0]
     pieces = local_time // (LANE * DEC)
-    taps = jnp.pad(filter_taps.astype(jnp.float32)[::-1], (DEC, SPAN - TAPS - DEC)).reshape(1, SPAN)
+    line = members // QUAD
     in_vmem = pl.BlockSpec(memory_space=pltpu.VMEM)
     low = pl.pallas_call(
         functools.partial(gather_kernel, members),
-        out_shape=jax.ShapeDtypeStruct((members, pieces, stations, LANE), jnp.bfloat16),
-        in_specs=[in_vmem] * 3,
-        out_specs=pl.BlockSpec(memory_space=pl.ANY),
+        out_shape=jax.ShapeDtypeStruct((members * pieces, ROWS, LANE), jnp.bfloat16),
+        in_specs=[
+            pl.BlockSpec(memory_space=pl.ANY),
+            in_vmem,
+            in_vmem,
+            pl.BlockSpec(memory_space=pltpu.SMEM),
+        ],
+        out_specs=in_vmem,
         scratch_shapes=[
+            pltpu.VMEM((stations, local_time), jnp.bfloat16),
             pltpu.VMEM((stations, TAPS), jnp.bfloat16),
-            pltpu.VMEM((pieces, stations, LANE), jnp.bfloat16),
+            pltpu.VMEM((line, pieces, stations, LANE), jnp.bfloat16),
+            pltpu.VMEM((stations // SB, SB, LANE), jnp.bfloat16),
+            pltpu.VMEM((3 * line * pieces, ROWS, LANE), jnp.bfloat16),
+            pltpu.SemaphoreType.DMA,
             pltpu.SemaphoreType.DMA((2,)),
-            pltpu.SemaphoreType.DMA,
-            pltpu.SemaphoreType.DMA((members,)),
-            pltpu.SemaphoreType.DMA((members,)),
+            pltpu.SemaphoreType.DMA((line * pieces,)),
+            pltpu.SemaphoreType.DMA((line * pieces,)),
+            pltpu.SemaphoreType.DMA((3 * line * pieces,)),
+            pltpu.SemaphoreType.DMA((members * pieces,)),
         ],
         compiler_params=pltpu.CompilerParams(
             collective_id=0, has_side_effects=True, vmem_limit_bytes=40 * 2**20
         ),
-    )(raw_traces, taps, station_order.reshape(stations, 1))
-    low = low.reshape(members * pieces, stations, LANE)
-    groups = jnp.concatenate([lax.dynamic_slice_in_dim(pairing, me, 1, 1)[:, 0], me[None].astype(jnp.int32)])
-    correlated = correlate(
-        window_starts,
-        groups,
-        low,
-        jnp.asarray(dft_table()),
-        jnp.asarray(lag_table(window_count)),
-    )
+    )(raw_traces, filter_taps.reshape(1, TAPS), station_order.reshape(1, stations), pairing)
+    correlated = correlate(window_starts, low, jnp.asarray(dft_table()), jnp.asarray(lag_table(window_count)))
     return correlated.reshape(ROUNDS, SB, SB, LAGS)
 
 

time: 54.4 us -> 49.5 us (0.910)
  Pallas kernels: 48.6 us -> 45.3 us
  local copies, waits for them, and re-layouts: 4.88 us -> 3.89 us
  other arithmetic: 0.62 us -> 0 us
    pallas_call x1, Pallas kernels: 25.3 us -> 23 us  [body(): pl.pallas_call(functools.partial(gather_kernel, members), out_shape=jax.S...]
    pallas_call x1, Pallas kernels: 23.3 us -> 22.3 us  [correlate(): pl.pallas_call(correlate_kernel, grid_spec=grid_spec, out_shape=jax.Shape...]
    rev x1 -> x0, local copies, waits for them, and re-layouts: 0.75 us -> none  [body(): filter_taps.astype(jnp.float32)[::-1]]
    concatenate x1 -> x0, other arithmetic: 0.62 us -> none  [body(): jnp.concatenate([lax.dynamic_slice_in_dim(pairing, me, 1, 1)[:, 0], me[No...]
    unnamed x6 -> x8, local copies, waits for them, and re-layouts: 3.06 us -> 3.23 us
where the time goes in v3:
time: 49.5 us; the launch traced here: 49.2 us
  Pallas kernels  45.3 us (92%)
  local copies, waits for them, and re-layouts  3.89 us (8%)
    pallas_call x1, Pallas kernels, body(): pl.pallas_call(functools.partial(gather_kernel, members), out_shape=jax.S...  23 us
    pallas_call x1, Pallas kernels, correlate(): pl.pallas_call(correlate_kernel, grid_spec=grid_spec, out_shape=jax.Shape...  22.3 us
    unnamed x8, local copies, waits for them, and re-layouts  3.23 us

profile of v3, /device:TPU:0, one launch (start us, length us, event | category | flops | bytes accessed | tf_op | source)
XLA Modules:
  0.0 49.2 jit_solution(305232311254150611)
XLA Ops:
  0.0 0.7 %reshape.9.taps_ref = bf16[1,256]{1,0:T(2,128)(2,1)S(1)} reshape(bf16[256]{0:T(256)(128)(2,1)} %param.8) | data formatting | bytes 1024 | tf_op jit(solution)/shard_map/reshape | solution.py:490
  0.7 0.0 copy-start.1
  0.7 1.0 %copy-done.1 = bf16[256,1024]{1,0:T(8,128)(2,1)S(1)} copy-done((bf16[256,1024]{1,0:T(8,128)(2,1)S(1)}, bf16[256,1024]{1,0:T(8,128)(2,1)}, u32[]{:S(2)}) %copy-start.1) | copy-done | bytes 524312
  1.7 0.0 copy-start.2
  1.7 0.7 %copy-done.2 = s32[4,16]{1,0:T(4,128)S(1)} copy-done((s32[4,16]{1,0:T(4,128)S(1)}, s32[4,16]{1,0:T(4,128)}, u32[]{:S(2)}) %copy-start.2) | copy-done | bytes 280
  2.4 0.0 copy-start.3
  2.4 0.7 %copy-done.3 = s32[256]{0:T(256)S(1)} copy-done((s32[256]{0:T(256)S(1)}, s32[256]{0:T(256)}, u32[]{:S(2)}) %copy-start.3) | copy-done | bytes 1048
  3.1 23.0 %shard_map.73.low_ref = bf16[32,80,128]{2,1,0:T(8,128)(2,1)S(1)} custom-call(bf16[256,1024]{1,0:T(8,128)(2,1)S(1)} %copy-done.1, bf16[1,256]{1,0:T(2,128)(2,1)S(1)} %reshape.9.taps_ref, s32[1,256]{1,0:T(1,128)S(1)} %bitcast.2, s32[4,16]{1,0:T(4,128)S(1)} %copy-done.2), custom_call_target="tpu_custom_call" | custom-call | tf_op jit(solution)/shard_map/pallas_call | solution.py:464
  26.1 0.0 copy-start
  26.1 0.8 %copy-done = bf16[32,80,128]{2,1,0:T(8,128)(2,1)} copy-done((bf16[32,80,128]{2,1,0:T(8,128)(2,1)}, bf16[32,80,128]{2,1,0:T(8,128)(2,1)S(1)}, u32[]{:S(2)}) %copy-start) | copy-done | bytes 655384
  26.9 22.3 %shard_map.74 = f32[4,256,256]{2,1,0:T(8,128)} custom-call(s32[16]{0:T(128)} %starts_ref.1, bf16[32,80,128]{2,1,0:T(8,128)(2,1)} %copy-done, bf16[2,1024,1024]{2,1,0:T(8,128)(2,1)} %constant.4.clone.dft_ref, bf16[2,256,1024]{2,1,0:T(8,128)(2,1)} %constant.5.clone.lag_ref), custom_call_target="tpu_custom_call" | custom-call | tf_op jit(solution)/shard_map/pallas_call | solution.py:449
Async XLA Ops:
  0.7 1.0 %copy-start.1 = (bf16[256,1024]{1,0:T(8,128)(2,1)S(1)}, bf16[256,1024]{1,0:T(8,128)(2,1)}, u32[]{:S(2)}) copy-start(bf16[256,1024]{1,0:T(8,128)(2,1)} %raw_ref.1) | copy-start | bytes 1572868
  1.7 0.7 %copy-start.2 = (s32[4,16]{1,0:T(4,128)S(1)}, s32[4,16]{1,0:T(4,128)}, u32[]{:S(2)}) copy-start(s32[4,16]{1,0:T(4,128)} %pairing_ref.1) | copy-start | bytes 772
  2.4 0.7 %copy-start.3 = (s32[256]{0:T(256)S(1)}, s32[256]{0:T(256)}, u32[]{:S(2)}) copy-start(s32[256]{0:T(256)} %param.9) | copy-start | bytes 3076
  26.1 0.8 %copy-start = (bf16[32,80,128]{2,1,0:T(8,128)(2,1)}, bf16[32,80,128]{2,1,0:T(8,128)(2,1)S(1)}, u32[]{:S(2)}) copy-start(bf16[32,80,128]{2,1,0:T(8,128)(2,1)S(1)} %shard_map.73.low_ref) | copy-start | bytes 1966084

commit v4 on v3

--- a/solution.py
+++ b/solution.py
@@ -23,8 +23,9 @@
 GROUPS = ROUNDS + 1
 ROWS = GROUPS * SB
 THEIRS = ROUNDS * SB
-FOLD = SEG // 2
-FT = 256
+FOLD = SEG // 4
+FT = 512
+HT = FT // 2
 TILES = BINS // FT
 PACK = 8
 NT = (((1,), (1,)), ((), ()))
@@ -32,18 +33,32 @@
 MESH = pl.DeviceIdType.MESH
 
 
+def taper_table():
+    sample = np.arange(-LANE, 7 * LANE)
+    return (0.5 - 0.5 * np.cos(sample * (2.0 * math.pi / SEG))).astype(np.float32).reshape(8, LANE)
+
+
 def dft_table():
     sample = np.arange(FOLD)
-    frequency = np.arange(BINS)
-    angles = (sample[None, :] * frequency[:, None] % SEG) * (2.0 * math.pi / SEG)
-    taper = (0.5 - 0.5 * np.cos(sample * (2.0 * math.pi / SEG)))[None, :]
-    both = np.stack([np.cos(angles) * taper, -np.sin(angles) * taper])
-    both[0, :, 0] = 1.0 - 2.0 * (frequency % 2)
-    return both.astype(np.float32).astype(ml_dtypes.bfloat16)
+    kinds = []
+    for wave in (np.cos, lambda a: -np.sin(a)):
+        for parity in range(2):
+            frequency = 2 * np.arange(BINS // 2) + parity
+            table = np.zeros((BINS // 2, FOLD + LANE))
+            table[:, :FOLD] = wave((sample[None, :] * frequency[:, None] % SEG) * (2.0 * math.pi / SEG))
+            middle = np.round(wave((frequency * FOLD % SEG) * (2.0 * math.pi / SEG)))
+            if wave is np.cos:
+                table[:, 0] = 0.5
+                table[:, FOLD] = middle
+            else:
+                table[:, 0] = middle
+            kinds.append(table)
+    return np.stack(kinds).astype(np.float32).astype(ml_dtypes.bfloat16)
 
 
 def lag_table(window_count):
-    frequency = np.arange(BINS)
+    frequency = 2 * np.arange(BINS // 2).reshape(TILES, 1, HT) + np.arange(2).reshape(1, 2, 1)
+    frequency = frequency.reshape(BINS)
     offset = np.arange(LAGS) - LAGS // 2 + SEG
     angles = (frequency[None, :] * offset[:, None] % SEG) * (2.0 * math.pi / SEG)
     scale = 1.0 / math.sqrt(BINS * window_count)
@@ -243,141 +258,179 @@
 def correlate_kernel(
     starts_ref,
     low_ref,
+    taper_ref,
+    dft_hbm,
+    lag_hbm,
+    out_ref,
     dft_ref,
     lag_ref,
-    out_ref,
     ahead,
     back,
-    even_theirs,
-    odd_theirs,
-    even_own,
-    odd_own,
+    theirs,
+    own,
     white_own,
     left,
     right,
     cross_real,
     cross_imag,
+    dft_sems,
+    lag_sem,
 ):
     tile = pl.program_id(0)
     planes = low_ref.shape[0]
     window_count = starts_ref.shape[0]
     lane = lax.broadcasted_iota(jnp.int32, (1, LANE), 1)
+    dft_copies = [
+        pltpu.make_async_copy(
+            dft_hbm.at[:, n * HT : (n + 1) * HT, :], dft_ref.at[:, n * HT : (n + 1) * HT, :], dft_sems.at[n]
+        )
+        for n in range(TILES)
+    ]
+    lag_copy = pltpu.make_async_copy(lag_hbm, lag_ref, lag_sem)
 
     @pl.when(tile == 0)
     def _():
+        for copy in dft_copies:
+            copy.start()
+        lag_copy.start()
         mirror = (
-            lax.broadcasted_iota(jnp.int32, (LANE, LANE), 0) + lax.broadcasted_iota(jnp.int32, (LANE, LANE), 1)
-            == LANE - 1
+            lax.broadcasted_iota(jnp.int32, (LANE, LANE), 0) + lax.broadcasted_iota(jnp.int32, (LANE, LANE), 1) == LANE
         ).astype(jnp.float32).astype(jnp.bfloat16)
-        back[0] = jnp.zeros((ROWS, LANE), jnp.float32)
 
         def one_plane(n, carry):
             samples = low_ref[n]
             ahead[n] = samples.astype(jnp.float32)
-            back[planes - n] = jnp.dot(samples, mirror, preferred_element_type=jnp.float32)
+            turned = jnp.dot(samples, mirror, preferred_element_type=jnp.float32)
+            later = low_ref[jnp.minimum(n + 1, planes - 1)].astype(jnp.float32)
+            later = jnp.where(n + 1 < planes, later, jnp.zeros_like(later))
+            back[planes - 1 - n] = jnp.where(lane == 0, later, turned)
             return carry
 
         lax.fori_loop(0, planes, one_plane, 0, unroll=8)
 
         def one_window(w, carry):
-            def shifted(ref, first):
-                plane = first // LANE
-                keep = LANE - first % LANE
-                shift = keep % LANE
-                now = pltpu.roll(ref[plane], shift, 1)
-                pieces = []
-                for piece in range(FOLD // LANE):
-                    later = pltpu.roll(ref[plane + piece + 1], shift, 1)
-                    pieces.append(jnp.where(lane < keep, now, later))
-                    now = later
-                return pieces, now
-
             start = starts_ref[w]
-            forward, middle = shifted(ahead, start)
-            backward, _ = shifted(back, planes * LANE - 1 - FOLD * 2 + LANE - start)
-            theirs = pl.ds(pl.multiple_of(w * THEIRS, SB), THEIRS)
-            own = pl.ds(pl.multiple_of(w * SB, SB), SB)
-            for piece, (a, b) in enumerate(zip(forward, backward)):
-                at = slice(piece * LANE, (piece + 1) * LANE)
-                even, odd = a + b, a - b
-                if piece == 0:
-                    even = jnp.where(lane == 0, middle, even)
-                even, odd = even.astype(jnp.bfloat16), odd.astype(jnp.bfloat16)
-                even_theirs[theirs, at] = even[:THEIRS]
-                odd_theirs[theirs, at] = odd[:THEIRS]
-                even_own[own, at] = even[THEIRS:]
-                odd_own[own, at] = odd[THEIRS:]
+            plane, rest = start // LANE, start % LANE
+            taper = taper_ref[...]
+            fore = pltpu.roll(taper, rest, 1)
+            hind = pltpu.roll(taper, (LANE - rest) % LANE, 1)
+            span = SEG // LANE
+            rise = [jnp.where(lane >= rest, fore[p + 1 : p + 2], fore[p : p + 1]) for p in range(FOLD // LANE + 1)]
+            fall = [
+                jnp.where(lane < LANE - rest, hind[p + 1 : p + 2], hind[p + 2 : p + 3]) for p in range(FOLD // LANE)
+            ]
+            at = pl.ds(pl.multiple_of(w * THEIRS, SB), THEIRS)
+            own_at = pl.ds(pl.multiple_of(w * SB, SB), SB)
+
+            def put(kind, p, values):
+                values = values.astype(jnp.bfloat16)
+                lanes = slice(p * LANE, (p + 1) * LANE)
+                theirs[kind, at, lanes] = values[:THEIRS]
+                own[kind, own_at, lanes] = values[THEIRS:]
+
+            last = FOLD // LANE
+            a = rise[last] * ahead[plane + last]
+            b = (1.0 - rise[last]) * ahead[plane + last + span // 2]
+            put(0, last, a + b)
+            middle = a - b
+            for p in range(FOLD // LANE):
+                first = ahead[plane + p]
+                if p == 0:
+                    first = jnp.where(lane < rest, ahead[jnp.minimum(plane + span, planes - 1)], first)
+                a = rise[p] * first
+                b = (1.0 - rise[p]) * ahead[plane + span // 2 + p]
+                c = fall[p] * back[planes - plane - span + p]
+                d = (1.0 - fall[p]) * back[planes - plane - span // 2 + p]
+                same, apart = a + b, a - b
+                same_turned, apart_turned = d + c, d - c
+                put(0, p, same + same_turned)
+                put(1, p, apart - apart_turned)
+                put(2, p, same - same_turned)
+                summed = apart + apart_turned
+                put(3, p, jnp.where(lane == 0, middle, summed) if p == 0 else summed)
             return carry
 
         lax.fori_loop(0, window_count, one_window, 0, unroll=2)
+
+    for n, copy in enumerate(dft_copies):
+
+        @pl.when(tile == n)
+        def _():
+            copy.wait()
 
     def dot_nt(a, b):
         return lax.dot_general(a, b, NT, preferred_element_type=jnp.float32)
 
+    bins = pl.ds(pl.multiple_of(tile * HT, HT), HT)
+    depth = (FOLD + LANE, FOLD, FOLD, FOLD)
     half = LANE // 2
-    pairs = window_count // 2
     wide = 2 * LANE
     first = lane < half
+    slots = LANE // PACK
+    turns = slots // 2
+    strip = BAND // 2
+    halves = HT // PACK
     for tile_pair in range(window_count * THEIRS // wide):
         at = slice(tile_pair * wide, (tile_pair + 1) * wide)
-        reals = dot_nt(dft_ref[0], even_theirs[at, :])
-        imags = dot_nt(dft_ref[1], odd_theirs[at, :])
-        for n in range(FT // BAND):
+        spectra = [dot_nt(dft_ref[k, bins, : depth[k]], theirs[k, at, : depth[k]]) for k in range(4)]
+        for n in range(HT // strip):
             for inner in range(wide // LANE):
-                pair = tile_pair * (wide // LANE) + inner
-                real, imag = (
-                    x[n * BAND : (n + 1) * BAND, inner * LANE : (inner + 1) * LANE] for x in (reals, imags)
-                )
-                level = jnp.sum(real * real + imag * imag, axis=0, keepdims=True)
+                parts = [x[n * strip : (n + 1) * strip, inner * LANE : (inner + 1) * LANE] for x in spectra]
+                power = sum(x * x for x in parts[1:]) + parts[0] * parts[0]
+                level = jnp.sum(power, axis=0, keepdims=True)
                 scale = lax.rsqrt(level * (1.0 / (2 * BAND)) + 1e-06)
-                real, imag = real * scale, imag * scale
-                real_turned, imag_turned = pltpu.roll(real, half, 1), pltpu.roll(imag, half, 1)
-                blocks = (
-                    (jnp.where(first, real, -imag_turned), jnp.where(first, real_turned, -imag)),
-                    (jnp.where(first, imag, real_turned), jnp.where(first, imag_turned, real)),
-                )
-                for c, block in enumerate(blocks):
-                    both = [x.reshape(BAND // PACK, 1, PACK, LANE) for x in block]
-                    both = jnp.concatenate(both, axis=1).reshape(BAND // PACK, 2 * PACK, LANE)
-                    row = (c * pairs + pair) * 2 * PACK
-                    right[n * (BAND // PACK) : (n + 1) * (BAND // PACK), row : row + 2 * PACK, :] = both.astype(
-                        jnp.bfloat16
+                for parity in range(2):
+                    real, imag = parts[parity] * scale, parts[2 + parity] * scale
+
+                    def stacked(x, y):
+                        both = [v.reshape(strip // PACK, 1, PACK, LANE) for v in (x, y)]
+                        both = jnp.concatenate(both, axis=1).reshape(strip * 2, LANE)
+                        return both.astype(jnp.bfloat16)
+
+                    plain, crossed = stacked(real, imag), stacked(-imag, real)
+                    turned = pltpu.roll(jnp.where(first, crossed, plain), half, 1)
+                    for k, block in enumerate((jnp.where(first, plain, turned), jnp.where(first, turned, crossed))):
+                        w = (tile_pair * (wide // LANE) + inner) * 2 + k
+                        for m in range(strip // PACK):
+                            group = n * (strip // PACK) + m
+                            turn = group % slots // 2
+                            row = w // turns * LANE + (w + turn) % turns * 2 * PACK
+                            right[parity * halves + group, row : row + 2 * PACK, :] = block[
+                                m * 2 * PACK : (m + 1) * 2 * PACK
+                            ]
+
+    spectra = [dot_nt(own[k, :, : depth[k]], dft_ref[k, bins, : depth[k]]) for k in range(4)]
+    power = sum(x * x for x in spectra[1:]) + spectra[0] * spectra[0]
+    same = (
+        lax.broadcasted_iota(jnp.int32, (HT, HT), 0) // strip == lax.broadcasted_iota(jnp.int32, (HT, HT), 1) // strip
+    ).astype(jnp.float32).astype(jnp.bfloat16)
+    level = jnp.dot(power.astype(jnp.bfloat16), same, preferred_element_type=jnp.float32)
+    scale = lax.rsqrt(level * (1.0 / (2 * BAND)) + 1e-06)
+    for k in range(4):
+        white_own[k] = (spectra[k] * scale).astype(jnp.bfloat16)
+
+    low_slot = lane // PACK % 2 == 0
+    for parity in range(2):
+        for part in range(HT // LANE):
+            for h in range(window_count // turns):
+                moved = [[], []]
+                for w in range(turns):
+                    row = (h * turns + w) * SB
+                    x = [
+                        white_own[2 * c + parity, row : row + SB, part * LANE : (part + 1) * LANE] for c in range(2)
+                    ]
+                    y = (
+                        jnp.where(low_slot, x[0], pltpu.roll(x[1], PACK, 1)),
+                        jnp.where(low_slot, pltpu.roll(x[0], LANE - PACK, 1), x[1]),
                     )
-
-    real, imag = dot_nt(even_own[...], dft_ref[0]), dot_nt(odd_own[...], dft_ref[1])
-    power = (real * real + imag * imag).astype(jnp.bfloat16)
-    same = (
-        lax.broadcasted_iota(jnp.int32, (FT, FT), 0) // BAND == lax.broadcasted_iota(jnp.int32, (FT, FT), 1) // BAND
-    ).astype(jnp.float32).astype(jnp.bfloat16)
-    level = jnp.dot(power, same, preferred_element_type=jnp.float32)
-    scale = lax.rsqrt(level * (1.0 / (2 * BAND)) + 1e-06)
-    white_own[0] = real * scale
-    white_own[1] = imag * scale
-
-    slots = LANE // PACK
-    for part in range(FT // LANE):
-        for c in range(2):
-            moved = [[], []]
-            for pair in range(pairs):
-                x = [
-                    white_own[c, (2 * pair + k) * SB : (2 * pair + k + 1) * SB, part * LANE : (part + 1) * LANE]
-                    for k in range(2)
-                ]
-                low_slot = lane // PACK % 2 == 0
-                y = (
-                    jnp.where(low_slot, x[0], pltpu.roll(x[1], PACK, 1)),
-                    jnp.where(low_slot, pltpu.roll(x[0], LANE - PACK, 1), x[1]),
-                )
-                for k in range(2):
-                    moved[k].append(pltpu.roll(y[k], 2 * PACK * pair, 1) if pair else y[k])
-            for slot in range(slots):
-                turn, k = slot // 2, slot % 2
-                joined = moved[k][0]
-                for pair in range(1, pairs):
-                    joined = jnp.where(lane // (2 * PACK) == (turn + pair) % (slots // 2), moved[k][pair], joined)
-                if turn:
-                    joined = pltpu.roll(joined, LANE - 2 * PACK * turn, 1)
-                left[part * slots + slot, c] = joined.astype(jnp.bfloat16)
+                    for k in range(2):
+                        moved[k].append(pltpu.roll(y[k], 2 * PACK * w, 1) if w else y[k])
+                for slot in range(slots):
+                    turn, k = slot // 2, slot % 2
+                    joined = moved[k][0]
+                    for w in range(1, turns):
+                        joined = jnp.where(lane // (2 * PACK) == (turn + w) % turns, moved[k][w], joined)
+                    left[parity * halves + part * slots + slot, h] = joined
 
     own_bin = lax.broadcasted_iota(jnp.int32, (PACK * SB, LANE), 0) // SB
     mask = (own_bin == lax.broadcasted_iota(jnp.int32, (PACK * SB, LANE), 1) % PACK).astype(jnp.float32).astype(
@@ -385,21 +438,22 @@
     )
 
     def one_group(n, carry):
-        masked = jnp.concatenate([jnp.concatenate([left[n, c]] * PACK, axis=0) * mask for c in range(2)], axis=1)
+        masked = jnp.concatenate([jnp.concatenate([left[n, h]] * PACK, axis=0) * mask for h in range(2)], axis=1)
         product = jnp.dot(masked, right[n], preferred_element_type=jnp.float32)
         product = product.reshape(PACK, 2, SB // 2, LANE)
-        first = lane < half
         a, b = product[:, 0].reshape(PACK * SB // 2, LANE), product[:, 1].reshape(PACK * SB // 2, LANE)
-        a_turned, b_turned = pltpu.roll(a, half, 1), pltpu.roll(b, half, 1)
+        turned = pltpu.roll(jnp.where(first, b, a), half, 1)
         at = pl.ds(pl.multiple_of((tile * (FT // PACK) + n) * PACK * SB // 2, PACK * SB // 2), PACK * SB // 2)
-        cross_real[at, :] = jnp.where(first, a, b_turned)
-        cross_imag[at, :] = jnp.where(first, a_turned, b)
+        cross_real[at, :] = jnp.where(first, a, turned)
+        cross_imag[at, :] = jnp.where(first, turned, b)
         return carry
 
     lax.fori_loop(0, FT // PACK, one_group, 0, unroll=16)
 
     @pl.when(tile == pl.num_programs(0) - 1)
     def _():
+        lag_copy.wait()
+
         def two_stations(n, carry):
             summed = None
             for k, cross in enumerate((cross_real, cross_imag)):
@@ -413,14 +467,14 @@
                 for h in range(2):
                     i = h * (SB // 2) + 2 * n + m
                     for r in range(ROUNDS):
-                        first = ((m * 2 + h) * ROUNDS + r) * SB
-                        out_ref[r, pl.ds(pl.multiple_of(i * SB, SB), SB), :] = turned[first : first + SB]
+                        row = ((m * 2 + h) * ROUNDS + r) * SB
+                        out_ref[r, pl.ds(pl.multiple_of(i * SB, SB), SB), :] = turned[row : row + SB]
             return carry
 
         lax.fori_loop(0, SB // 4, two_stations, 0, unroll=True)
 
 
-def correlate(window_starts, low, dft, lag):
+def correlate(window_starts, low, taper, dft, lag):
     window_count = window_starts.shape[0]
     planes = low.shape[0]
     grid_spec = pltpu.PrefetchScalarGridSpec(
@@ -428,30 +482,33 @@
         grid=(TILES,),
         in_specs=[
             pl.BlockSpec((planes, ROWS, LANE), lambda n, *_: (0, 0, 0)),
-            pl.BlockSpec((2, FT, FOLD), lambda n, *_: (0, n, 0)),
-            pl.BlockSpec((2, LAGS, BINS), lambda n, *_: (0, 0, 0)),
+            pl.BlockSpec((8, LANE), lambda n, *_: (0, 0)),
+            pl.BlockSpec(memory_space=pl.ANY),
+            pl.BlockSpec(memory_space=pl.ANY),
         ],
         out_specs=pl.BlockSpec((ROUNDS, SB * SB, LAGS), lambda n, *_: (0, 0, 0)),
         scratch_shapes=[
+            pltpu.VMEM(dft.shape, jnp.bfloat16),
+            pltpu.VMEM(lag.shape, jnp.bfloat16),
             pltpu.VMEM((planes, ROWS, LANE), jnp.float32),
-            pltpu.VMEM((planes + 1, ROWS, LANE), jnp.float32),
-            pltpu.VMEM((window_count * THEIRS, FOLD), jnp.bfloat16),
-            pltpu.VMEM((window_count * THEIRS, FOLD), jnp.bfloat16),
-            pltpu.VMEM((window_count * SB, FOLD), jnp.bfloat16),
-            pltpu.VMEM((window_count * SB, FOLD), jnp.bfloat16),
-            pltpu.VMEM((2, window_count * SB, FT), jnp.float32),
+            pltpu.VMEM((planes, ROWS, LANE), jnp.float32),
+            pltpu.VMEM((4, window_count * THEIRS, FOLD + LANE), jnp.bfloat16),
+            pltpu.VMEM((4, window_count * SB, FOLD + LANE), jnp.bfloat16),
+            pltpu.VMEM((4, window_count * SB, HT), jnp.bfloat16),
             pltpu.VMEM((FT // PACK, 2, SB, LANE), jnp.bfloat16),
             pltpu.VMEM((FT // PACK, 2 * LANE, LANE), jnp.bfloat16),
             pltpu.VMEM((BINS * SB // 2, LANE), jnp.float32),
             pltpu.VMEM((BINS * SB // 2, LANE), jnp.float32),
+            pltpu.SemaphoreType.DMA((TILES,)),
+            pltpu.SemaphoreType.DMA,
         ],
     )
     return pl.pallas_call(
         correlate_kernel,
         grid_spec=grid_spec,
         out_shape=jax.ShapeDtypeStruct((ROUNDS, SB * SB, LAGS), jnp.float32),
-        compiler_params=pltpu.CompilerParams(vmem_limit_bytes=56 * 2**20),
-    )(window_starts, low, dft, lag)
+        compiler_params=pltpu.CompilerParams(vmem_limit_bytes=60 * 2**20),
+    )(window_starts, low, taper, dft, lag)
 
 
 def body(raw_traces, filter_taps, station_order, window_starts, pairing):
@@ -485,10 +542,16 @@
             pltpu.SemaphoreType.DMA((members * pieces,)),
         ],
         compiler_params=pltpu.CompilerParams(
-            collective_id=0, has_side_effects=True, vmem_limit_bytes=40 * 2**20
+            collective_id=0, has_side_effects=True, vmem_limit_bytes=60 * 2**20
         ),
     )(raw_traces, filter_taps.reshape(1, TAPS), station_order.reshape(1, stations), pairing)
-    correlated = correlate(window_starts, low, jnp.asarray(dft_table()), jnp.asarray(lag_table(window_count)))
+    correlated = correlate(
+        window_starts,
+        low,
+        jnp.asarray(taper_table()),
+        jnp.asarray(dft_table()),
+        jnp.asarray(lag_table(window_count)),
+    )
     return correlated.reshape(ROUNDS, SB, SB, LAGS)
 
 

time: 49.5 us -> 42.4 us (0.86)
  Pallas kernels: 45.3 us -> 41 us
  local copies, waits for them, and re-layouts: 3.89 us -> 1.22 us
    pallas_call x1, Pallas kernels: 22.3 us -> 17 us  [correlate(): pl.pallas_call(correlate_kernel, grid_spec=grid_spec, out_shape=jax.Shape...]
    unnamed x8 -> x0, local copies, waits for them, and re-layouts: 3.23 us -> none
    pallas_call x1, Pallas kernels: 23 us -> 24 us  [body(): pl.pallas_call(functools.partial(gather_kernel, members), out_shape=jax.S...]
    reshape x1, local copies, waits for them, and re-layouts: 0.66 us -> 1.22 us  [body(): filter_taps.reshape(1, TAPS)]
where the time goes in v4:
time: 42.4 us; the launch traced here: 42.2 us
  Pallas kernels  41 us (97%)
  local copies, waits for them, and re-layouts  1.22 us (3%)
    pallas_call x1, Pallas kernels, body(): pl.pallas_call(functools.partial(gather_kernel, members), out_shape=jax.S...  24 us
    pallas_call x1, Pallas kernels, correlate(): pl.pallas_call(correlate_kernel, grid_spec=grid_spec, out_shape=jax.Shape...  17 us
    reshape x1, local copies, waits for them, and re-layouts, body(): filter_taps.reshape(1, TAPS)  1.22 us

profile of v4, /device:TPU:0, one launch (start us, length us, event | category | flops | bytes accessed | tf_op | source)
XLA Modules:
  0.0 42.2 jit_solution(3608017387840804101)
XLA Ops:
  0.0 1.2 %reshape.9.taps_ref = bf16[1,256]{1,0:T(2,128)(2,1)} reshape(bf16[256]{0:T(256)(128)(2,1)} %param.9) | data formatting | bytes 1024 | tf_op jit(solution)/shard_map/reshape | solution.py:547
  1.2 24.0 %shard_map.82.low_ref = bf16[32,80,128]{2,1,0:T(8,128)(2,1)} custom-call(bf16[256,1024]{1,0:T(8,128)(2,1)} %raw_ref.1, bf16[1,256]{1,0:T(2,128)(2,1)} %reshape.9.taps_ref, s32[1,256]{1,0:T(1,128)} %bitcast.2, s32[4,16]{1,0:T(4,128)} %pairing_ref.1), custom_call_target="tpu_custom_call" | custom-call | tf_op jit(solution)/shard_map/pallas_call | solution.py:521
  25.2 17.0 %shard_map.83 = f32[4,256,256]{2,1,0:T(8,128)} custom-call(s32[16]{0:T(128)} %starts_ref.1, bf16[32,80,128]{2,1,0:T(8,128)(2,1)} %shard_map.82.low_ref, f32[8,128]{1,0:T(8,128)} %constant.6.clone.taper_ref, bf16[4,512,640]{2,1,0:T(8,128)(2,1)} %constant.7.clone.dft_hbm, bf16[2,256,1024]{2,1,0:T(8,128)(2,1)} %constant.8.clone.lag_hbm), custom_call_target="tpu_custom_call" | custom-call | tf_op jit(solution)/shard_map/pallas_call | solution.py:506

commit v5 on v4

--- a/solution.py
+++ b/solution.py
@@ -74,6 +74,7 @@
     pairing_ref,
     out_ref,
     raw,
+    tail,
     halo,
     column,
     private,
@@ -95,27 +96,33 @@
     others = (across, across + turn, twin)
     after, before = lax.rem(me + 1, members), lax.rem(me + members - 1, members)
 
-    def nearest(n):
-        chosen = None
-        for r in range(line):
-            order = sorted((x for x in range(line) if x != r), key=lambda x: abs(x - r))
-            chosen = order[n] if chosen is None else jnp.where(rank == r, order[n], chosen)
+    def of_rank(choose):
+        chosen = choose(0)
+        for r in range(1, line):
+            chosen = jnp.where(rank == r, choose(r), chosen)
         return chosen
 
-    line_order = [nearest(n) for n in range(line - 1)]
+    def arrivals(r):
+        known = sorted((abs(x - r), -piece, x) for x in range(line) if x != r for piece in range(pieces))
+        return [(x, -negative) for _, negative, x in known]
+
+    expected = [
+        (of_rank(lambda r: arrivals(r)[n][0]), of_rank(lambda r: arrivals(r)[n][1]))
+        for n in range((line - 1) * pieces)
+    ]
 
     raw_copy = pltpu.make_async_copy(raw_ref, raw, raw_sem)
     raw_copy.start()
 
     barrier = pltpu.get_barrier_semaphore()
-    greeted = [r * QUAD + lead for r in line_order] + list(others) + [after, before]
+    greeted = [lax.rem(rank + n, line) * QUAD + lead for n in range(1, line)] + list(others) + [after, before]
     for peer in greeted:
         pl.semaphore_signal(barrier, inc=1, device_id={"sta": peer}, device_id_type=MESH)
 
     mirror = (
         lax.broadcasted_iota(jnp.int32, (TAPS, TAPS), 0) + lax.broadcasted_iota(jnp.int32, (TAPS, TAPS), 1) == TAPS - 1
     ).astype(jnp.float32).astype(jnp.bfloat16)
-    taps = jnp.broadcast_to(taps_ref[...].astype(jnp.float32), (SB, TAPS)).astype(jnp.bfloat16)
+    taps = jnp.broadcast_to(taps_ref[...].astype(jnp.float32).reshape(1, TAPS), (SB, TAPS)).astype(jnp.bfloat16)
     taps = jnp.dot(taps, mirror, preferred_element_type=jnp.float32)[:1]
     banded = jnp.concatenate([taps, jnp.zeros((1, SPAN - TAPS), jnp.float32)], axis=1)
     banded = jnp.broadcast_to(banded, (LANE, SPAN))
@@ -123,10 +130,21 @@
     picks = (lax.broadcasted_iota(jnp.int32, (stations, stations), 0) == order_ref[...]).astype(jnp.float32)
     picks = picks.T.astype(jnp.bfloat16)
 
+    dims = (((1,), (1,)), ((), ()))
+    lane = lax.broadcasted_iota(jnp.int32, (1, LANE), 1)
+    half = LANE // 2
+    raw_copy.wait()
+    spilled = lax.dot_general(
+        raw[:, local_time - TAPS :], banded[:, :TAPS], dims, preferred_element_type=jnp.float32
+    )
+    tail[...] = jnp.where(
+        lane < half, spilled[: stations // 2], pltpu.roll(spilled[stations // 2 :], half, 1)
+    ).astype(jnp.bfloat16)
+
     pl.semaphore_wait(barrier, len(greeted))
 
     halo_copy = pltpu.make_async_remote_copy(
-        src_ref=raw_ref.at[:, local_time - TAPS :],
+        src_ref=tail,
         dst_ref=halo,
         send_sem=halo_sems.at[0],
         recv_sem=halo_sems.at[1],
@@ -142,16 +160,22 @@
         return pltpu.make_async_remote_copy(
             src_ref=column.at[source, piece],
             dst_ref=column.at[source, piece],
-            send_sem=line_send.at[piece * line + n],
+            send_sem=line_send.at[n],
             recv_sem=line_recv.at[source * pieces + piece],
             device_id={"sta": peer * QUAD + lead},
             device_id_type=MESH,
         )
 
-    at_end = (rank == 0) | (rank == line - 1)
-    beside_end = (rank == 1) | (rank == line - 2)
-    far_end = jnp.where(rank == 1, 0, line - 1)
-    relayed = line > 3
+    passed = []
+
+    def pass_on(source, piece, ahead, there):
+        copy = line_copy(source, piece, len(passed), rank + ahead)
+        passed.append((copy, there))
+
+        @pl.when(there)
+        def _():
+            copy.start()
+
     picks_sent = []
 
     def share(source, piece, samples):
@@ -161,11 +185,10 @@
             blocks = [pairing_ref[r, peer] for r in range(ROUNDS)] + [peer]
             slot = len(picks_sent)
             for g, block in enumerate(blocks):
-                chosen = private[block]
                 if k < len(others):
-                    picked[slot, g * SB : (g + 1) * SB, :] = chosen
+                    picked[slot, g * SB : (g + 1) * SB, :] = private[block]
                 else:
-                    out_ref[plane, g * SB : (g + 1) * SB, :] = chosen
+                    out_ref[plane, g * SB : (g + 1) * SB, :] = private[block]
             if k < len(others):
                 copy = pltpu.make_async_remote_copy(
                     src_ref=picked.at[slot],
@@ -178,26 +201,23 @@
                 copy.start()
                 picks_sent.append(copy)
 
-    dims = (((1,), (1,)), ((), ()))
-
-    def filtered(piece, samples):
-        summed = lax.dot_general(samples, banded, dims, preferred_element_type=jnp.float32)
+    def filtered(piece, first, spill=None):
+        summed = lax.dot_general(
+            raw[:, max(first, 0) : first + SPAN],
+            banded[:, max(-first, 0) :],
+            dims,
+            preferred_element_type=jnp.float32,
+        )
+        if spill is not None:
+            summed = summed + spill
         ordered = jnp.dot(picks, summed.astype(jnp.bfloat16), preferred_element_type=jnp.float32).astype(jnp.bfloat16)
         column[rank, piece] = ordered
-        for n, peer in enumerate(line_order):
-            if n == line - 2 and relayed:
-
-                @pl.when(jnp.logical_not(at_end))
-                def _():
-                    line_copy(rank, piece, n, peer).start()
-            else:
-                line_copy(rank, piece, n, peer).start()
+        pass_on(rank, piece, 1, rank < line - 1)
+        pass_on(rank, piece, -1, rank > 0)
         share(rank, piece, ordered)
 
-    raw_copy.wait()
     for piece in range(pieces - 1, 0, -1):
-        first = piece * LANE * DEC - TAPS
-        filtered(piece, raw[:, first : first + SPAN])
+        filtered(piece, piece * LANE * DEC - TAPS)
 
     @pl.when(me > 0)
     def _():
@@ -207,18 +227,20 @@
     def _():
         halo[...] = jnp.zeros_like(halo)
 
-    filtered(0, jnp.concatenate([halo[...], raw[:, : LANE * DEC]], axis=1))
-
-    for n, source in enumerate(line_order):
-        for piece in range(pieces - 1, -1, -1):
-            line_copy(source, piece, n, source).wait_recv()
-            if n == line - 2 and relayed:
-
-                @pl.when(beside_end)
-                def _():
-                    line_copy(source, piece, line - 1, far_end).start()
-
-            share(source, piece, column[source, piece])
+    spill = halo[...].astype(jnp.float32)
+    spill = [jnp.where(lane < half, x, 0.0) for x in (spill, pltpu.roll(spill, half, 1))]
+    filtered(0, -TAPS, jnp.concatenate(spill, axis=0))
+
+    for source, piece in expected:
+        from_below = source < rank
+        line_copy(source, piece, 0, source).wait_recv()
+        pass_on(
+            source,
+            piece,
+            jnp.where(from_below, 1, -1),
+            (from_below & (rank < line - 1)) | (jnp.logical_not(from_below) & (rank > 0)),
+        )
+        share(source, piece, column[source, piece])
 
     for source in range(line):
         for piece in range(pieces):
@@ -235,20 +257,11 @@
                 ).wait_recv()
     for copy in picks_sent:
         copy.wait_send()
-    for piece in range(pieces):
-        for n, peer in enumerate(line_order):
-            if n == line - 2 and relayed:
-
-                @pl.when(jnp.logical_not(at_end))
-                def _():
-                    line_copy(rank, piece, n, peer).wait_send()
-            else:
-                line_copy(rank, piece, n, peer).wait_send()
-        if relayed:
-
-            @pl.when(beside_end)
-            def _():
-                line_copy(line_order[-1], piece, line - 1, far_end).wait_send()
+    for copy, there in passed:
+
+        @pl.when(there)
+        def _():
+            copy.wait_send()
 
     @pl.when(me < members - 1)
     def _():
@@ -530,13 +543,14 @@
         out_specs=in_vmem,
         scratch_shapes=[
             pltpu.VMEM((stations, local_time), jnp.bfloat16),
-            pltpu.VMEM((stations, TAPS), jnp.bfloat16),
+            pltpu.VMEM((stations // 2, LANE), jnp.bfloat16),
+            pltpu.VMEM((stations // 2, LANE), jnp.bfloat16),
             pltpu.VMEM((line, pieces, stations, LANE), jnp.bfloat16),
             pltpu.VMEM((stations // SB, SB, LANE), jnp.bfloat16),
             pltpu.VMEM((3 * line * pieces, ROWS, LANE), jnp.bfloat16),
             pltpu.SemaphoreType.DMA,
             pltpu.SemaphoreType.DMA((2,)),
-            pltpu.SemaphoreType.DMA((line * pieces,)),
+            pltpu.SemaphoreType.DMA(((line + 1) * pieces,)),
             pltpu.SemaphoreType.DMA((line * pieces,)),
             pltpu.SemaphoreType.DMA((3 * line * pieces,)),
             pltpu.SemaphoreType.DMA((members * pieces,)),
@@ -544,7 +558,7 @@
         compiler_params=pltpu.CompilerParams(
             collective_id=0, has_side_effects=True, vmem_limit_bytes=60 * 2**20
         ),
-    )(raw_traces, filter_taps.reshape(1, TAPS), station_order.reshape(1, stations), pairing)
+    )(raw_traces, filter_taps, station_order.reshape(1, stations), pairing)
     correlated = correlate(
         window_starts,
         low,

time: 42.4 us -> 39.7 us (0.936)
  Pallas kernels: 41 us -> 39.5 us
  local copies, waits for them, and re-layouts: 1.22 us -> 0 us
    pallas_call x1, Pallas kernels: 24 us -> 22.5 us  [body(): pl.pallas_call(functools.partial(gather_kernel, members), out_shape=jax.S...]
    reshape x1 -> x0, local copies, waits for them, and re-layouts: 1.22 us -> none  [body(): filter_taps.reshape(1, TAPS)]
where the time goes in v5:
time: 39.7 us; the launch traced here: 39.5 us
  Pallas kernels  39.5 us (99%)
    pallas_call x1, Pallas kernels, body(): pl.pallas_call(functools.partial(gather_kernel, members), out_shape=jax.S...  22.5 us
    pallas_call x1, Pallas kernels, correlate(): pl.pallas_call(correlate_kernel, grid_spec=grid_spec, out_shape=jax.Shape...  17 us

profile of v5, /device:TPU:0, one launch (start us, length us, event | category | flops | bytes accessed | tf_op | source)
XLA Modules:
  0.0 39.5 jit_solution(13141301666823174032)
XLA Ops:
  0.0 22.5 %shard_map.82.low_ref = bf16[32,80,128]{2,1,0:T(8,128)(2,1)} custom-call(bf16[256,1024]{1,0:T(8,128)(2,1)} %raw_ref.1, bf16[256]{0:T(256)(128)(2,1)} %taps_ref.1, s32[1,256]{1,0:T(1,128)} %bitcast.2, s32[4,16]{1,0:T(4,128)} %pairing_ref.1), custom_call_target="tpu_custom_call" | custom-call | tf_op jit(solution)/shard_map/pallas_call | solution.py:534
  22.5 17.0 %shard_map.83 = f32[4,256,256]{2,1,0:T(8,128)} custom-call(s32[16]{0:T(128)} %starts_ref.1, bf16[32,80,128]{2,1,0:T(8,128)(2,1)} %shard_map.82.low_ref, f32[8,128]{1,0:T(8,128)} %constant.6.clone.taper_ref, bf16[4,512,640]{2,1,0:T(8,128)(2,1)} %constant.7.clone.dft_hbm, bf16[2,256,1024]{2,1,0:T(8,128)(2,1)} %constant.8.clone.lag_hbm), custom_call_target="tpu_custom_call" | custom-call | tf_op jit(solution)/shard_map/pallas_call | solution.py:519

commit v6 on v5

--- a/solution.py
+++ b/solution.py
@@ -274,6 +274,7 @@
     taper_ref,
     dft_hbm,
     lag_hbm,
+    out_hbm,
     out_ref,
     dft_ref,
     lag_ref,
@@ -288,8 +289,8 @@
     cross_imag,
     dft_sems,
     lag_sem,
+    out_sems,
 ):
-    tile = pl.program_id(0)
     planes = low_ref.shape[0]
     window_count = starts_ref.shape[0]
     lane = lax.broadcasted_iota(jnp.int32, (1, LANE), 1)
@@ -301,80 +302,71 @@
     ]
     lag_copy = pltpu.make_async_copy(lag_hbm, lag_ref, lag_sem)
 
-    @pl.when(tile == 0)
-    def _():
-        for copy in dft_copies:
-            copy.start()
-        lag_copy.start()
-        mirror = (
-            lax.broadcasted_iota(jnp.int32, (LANE, LANE), 0) + lax.broadcasted_iota(jnp.int32, (LANE, LANE), 1) == LANE
-        ).astype(jnp.float32).astype(jnp.bfloat16)
-
-        def one_plane(n, carry):
-            samples = low_ref[n]
-            ahead[n] = samples.astype(jnp.float32)
-            turned = jnp.dot(samples, mirror, preferred_element_type=jnp.float32)
-            later = low_ref[jnp.minimum(n + 1, planes - 1)].astype(jnp.float32)
-            later = jnp.where(n + 1 < planes, later, jnp.zeros_like(later))
-            back[planes - 1 - n] = jnp.where(lane == 0, later, turned)
-            return carry
-
-        lax.fori_loop(0, planes, one_plane, 0, unroll=8)
-
-        def one_window(w, carry):
-            start = starts_ref[w]
-            plane, rest = start // LANE, start % LANE
-            taper = taper_ref[...]
-            fore = pltpu.roll(taper, rest, 1)
-            hind = pltpu.roll(taper, (LANE - rest) % LANE, 1)
-            span = SEG // LANE
-            rise = [jnp.where(lane >= rest, fore[p + 1 : p + 2], fore[p : p + 1]) for p in range(FOLD // LANE + 1)]
-            fall = [
-                jnp.where(lane < LANE - rest, hind[p + 1 : p + 2], hind[p + 2 : p + 3]) for p in range(FOLD // LANE)
-            ]
-            at = pl.ds(pl.multiple_of(w * THEIRS, SB), THEIRS)
-            own_at = pl.ds(pl.multiple_of(w * SB, SB), SB)
-
-            def put(kind, p, values):
-                values = values.astype(jnp.bfloat16)
-                lanes = slice(p * LANE, (p + 1) * LANE)
-                theirs[kind, at, lanes] = values[:THEIRS]
-                own[kind, own_at, lanes] = values[THEIRS:]
-
-            last = FOLD // LANE
-            a = rise[last] * ahead[plane + last]
-            b = (1.0 - rise[last]) * ahead[plane + last + span // 2]
-            put(0, last, a + b)
-            middle = a - b
-            for p in range(FOLD // LANE):
-                first = ahead[plane + p]
-                if p == 0:
-                    first = jnp.where(lane < rest, ahead[jnp.minimum(plane + span, planes - 1)], first)
-                a = rise[p] * first
-                b = (1.0 - rise[p]) * ahead[plane + span // 2 + p]
-                c = fall[p] * back[planes - plane - span + p]
-                d = (1.0 - fall[p]) * back[planes - plane - span // 2 + p]
-                same, apart = a + b, a - b
-                same_turned, apart_turned = d + c, d - c
-                put(0, p, same + same_turned)
-                put(1, p, apart - apart_turned)
-                put(2, p, same - same_turned)
-                summed = apart + apart_turned
-                put(3, p, jnp.where(lane == 0, middle, summed) if p == 0 else summed)
-            return carry
-
-        lax.fori_loop(0, window_count, one_window, 0, unroll=2)
-
-    for n, copy in enumerate(dft_copies):
-
-        @pl.when(tile == n)
-        def _():
-            copy.wait()
+    for copy in dft_copies:
+        copy.start()
+    lag_copy.start()
+    mirror = (
+        lax.broadcasted_iota(jnp.int32, (LANE, LANE), 0) + lax.broadcasted_iota(jnp.int32, (LANE, LANE), 1) == LANE
+    ).astype(jnp.float32).astype(jnp.bfloat16)
+
+    def one_plane(n, carry):
+        samples = low_ref[n]
+        ahead[n] = samples.astype(jnp.float32)
+        turned = jnp.dot(samples, mirror, preferred_element_type=jnp.float32)
+        later = low_ref[jnp.minimum(n + 1, planes - 1)].astype(jnp.float32)
+        later = jnp.where(n + 1 < planes, later, jnp.zeros_like(later))
+        back[planes - 1 - n] = jnp.where(lane == 0, later, turned)
+        return carry
+
+    lax.fori_loop(0, planes, one_plane, 0, unroll=16)
+
+    def one_window(w, carry):
+        start = starts_ref[w]
+        plane, rest = start // LANE, start % LANE
+        taper = taper_ref[...]
+        fore = pltpu.roll(taper, rest, 1)
+        hind = pltpu.roll(taper, (LANE - rest) % LANE, 1)
+        span = SEG // LANE
+        rise = [jnp.where(lane >= rest, fore[p + 1 : p + 2], fore[p : p + 1]) for p in range(FOLD // LANE + 1)]
+        fall = [
+            jnp.where(lane < LANE - rest, hind[p + 1 : p + 2], hind[p + 2 : p + 3]) for p in range(FOLD // LANE)
+        ]
+        at = pl.ds(pl.multiple_of(w * THEIRS, SB), THEIRS)
+        own_at = pl.ds(pl.multiple_of(w * SB, SB), SB)
+
+        def put(kind, p, values):
+            values = values.astype(jnp.bfloat16)
+            lanes = slice(p * LANE, (p + 1) * LANE)
+            theirs[kind, at, lanes] = values[:THEIRS]
+            own[kind, own_at, lanes] = values[THEIRS:]
+
+        last = FOLD // LANE
+        a = rise[last] * ahead[plane + last]
+        b = (1.0 - rise[last]) * ahead[plane + last + span // 2]
+        put(0, last, a + b)
+        middle = a - b
+        for p in range(FOLD // LANE):
+            first = ahead[plane + p]
+            if p == 0:
+                first = jnp.where(lane < rest, ahead[jnp.minimum(plane + span, planes - 1)], first)
+            a = rise[p] * first
+            b = (1.0 - rise[p]) * ahead[plane + span // 2 + p]
+            c = fall[p] * back[planes - plane - span + p]
+            d = (1.0 - fall[p]) * back[planes - plane - span // 2 + p]
+            same, apart = a + b, a - b
+            same_turned, apart_turned = d + c, d - c
+            put(0, p, same + same_turned)
+            put(1, p, apart - apart_turned)
+            put(2, p, same - same_turned)
+            summed = apart + apart_turned
+            put(3, p, jnp.where(lane == 0, middle, summed) if p == 0 else summed)
+        return carry
+
+    lax.fori_loop(0, window_count, one_window, 0, unroll=8)
 
     def dot_nt(a, b):
         return lax.dot_general(a, b, NT, preferred_element_type=jnp.float32)
 
-    bins = pl.ds(pl.multiple_of(tile * HT, HT), HT)
     depth = (FOLD + LANE, FOLD, FOLD, FOLD)
     half = LANE // 2
     wide = 2 * LANE
@@ -383,143 +375,154 @@
     turns = slots // 2
     strip = BAND // 2
     halves = HT // PACK
-    for tile_pair in range(window_count * THEIRS // wide):
-        at = slice(tile_pair * wide, (tile_pair + 1) * wide)
-        spectra = [dot_nt(dft_ref[k, bins, : depth[k]], theirs[k, at, : depth[k]]) for k in range(4)]
-        for n in range(HT // strip):
-            for inner in range(wide // LANE):
-                parts = [x[n * strip : (n + 1) * strip, inner * LANE : (inner + 1) * LANE] for x in spectra]
-                power = sum(x * x for x in parts[1:]) + parts[0] * parts[0]
-                level = jnp.sum(power, axis=0, keepdims=True)
-                scale = lax.rsqrt(level * (1.0 / (2 * BAND)) + 1e-06)
-                for parity in range(2):
-                    real, imag = parts[parity] * scale, parts[2 + parity] * scale
-
-                    def stacked(x, y):
-                        both = [v.reshape(strip // PACK, 1, PACK, LANE) for v in (x, y)]
-                        both = jnp.concatenate(both, axis=1).reshape(strip * 2, LANE)
-                        return both.astype(jnp.bfloat16)
-
-                    plain, crossed = stacked(real, imag), stacked(-imag, real)
-                    turned = pltpu.roll(jnp.where(first, crossed, plain), half, 1)
-                    for k, block in enumerate((jnp.where(first, plain, turned), jnp.where(first, turned, crossed))):
-                        w = (tile_pair * (wide // LANE) + inner) * 2 + k
-                        for m in range(strip // PACK):
-                            group = n * (strip // PACK) + m
-                            turn = group % slots // 2
-                            row = w // turns * LANE + (w + turn) % turns * 2 * PACK
-                            right[parity * halves + group, row : row + 2 * PACK, :] = block[
-                                m * 2 * PACK : (m + 1) * 2 * PACK
-                            ]
-
-    spectra = [dot_nt(own[k, :, : depth[k]], dft_ref[k, bins, : depth[k]]) for k in range(4)]
-    power = sum(x * x for x in spectra[1:]) + spectra[0] * spectra[0]
-    same = (
-        lax.broadcasted_iota(jnp.int32, (HT, HT), 0) // strip == lax.broadcasted_iota(jnp.int32, (HT, HT), 1) // strip
-    ).astype(jnp.float32).astype(jnp.bfloat16)
-    level = jnp.dot(power.astype(jnp.bfloat16), same, preferred_element_type=jnp.float32)
-    scale = lax.rsqrt(level * (1.0 / (2 * BAND)) + 1e-06)
-    for k in range(4):
-        white_own[k] = (spectra[k] * scale).astype(jnp.bfloat16)
-
-    low_slot = lane // PACK % 2 == 0
-    for parity in range(2):
-        for part in range(HT // LANE):
-            for h in range(window_count // turns):
-                moved = [[], []]
-                for w in range(turns):
-                    row = (h * turns + w) * SB
-                    x = [
-                        white_own[2 * c + parity, row : row + SB, part * LANE : (part + 1) * LANE] for c in range(2)
-                    ]
-                    y = (
-                        jnp.where(low_slot, x[0], pltpu.roll(x[1], PACK, 1)),
-                        jnp.where(low_slot, pltpu.roll(x[0], LANE - PACK, 1), x[1]),
-                    )
-                    for k in range(2):
-                        moved[k].append(pltpu.roll(y[k], 2 * PACK * w, 1) if w else y[k])
-                for slot in range(slots):
-                    turn, k = slot // 2, slot % 2
-                    joined = moved[k][0]
-                    for w in range(1, turns):
-                        joined = jnp.where(lane // (2 * PACK) == (turn + w) % turns, moved[k][w], joined)
-                    left[parity * halves + part * slots + slot, h] = joined
-
     own_bin = lax.broadcasted_iota(jnp.int32, (PACK * SB, LANE), 0) // SB
     mask = (own_bin == lax.broadcasted_iota(jnp.int32, (PACK * SB, LANE), 1) % PACK).astype(jnp.float32).astype(
         jnp.bfloat16
     )
 
-    def one_group(n, carry):
-        masked = jnp.concatenate([jnp.concatenate([left[n, h]] * PACK, axis=0) * mask for h in range(2)], axis=1)
-        product = jnp.dot(masked, right[n], preferred_element_type=jnp.float32)
+    def one_group(tile, n):
+        masked = jnp.concatenate([jnp.concatenate([left[tile, n, h]] * PACK, axis=0) * mask for h in range(2)], axis=1)
+        product = jnp.dot(masked, right[tile, n], preferred_element_type=jnp.float32)
         product = product.reshape(PACK, 2, SB // 2, LANE)
         a, b = product[:, 0].reshape(PACK * SB // 2, LANE), product[:, 1].reshape(PACK * SB // 2, LANE)
         turned = pltpu.roll(jnp.where(first, b, a), half, 1)
-        at = pl.ds(pl.multiple_of((tile * (FT // PACK) + n) * PACK * SB // 2, PACK * SB // 2), PACK * SB // 2)
+        row = (tile * (FT // PACK) + n) * PACK * SB // 2
+        at = pl.ds(row if isinstance(n, int) else pl.multiple_of(row, PACK * SB // 2), PACK * SB // 2)
         cross_real[at, :] = jnp.where(first, a, turned)
         cross_imag[at, :] = jnp.where(first, turned, b)
-        return carry
-
-    lax.fori_loop(0, FT // PACK, one_group, 0, unroll=16)
-
-    @pl.when(tile == pl.num_programs(0) - 1)
-    def _():
-        lag_copy.wait()
-
-        def two_stations(n, carry):
-            summed = None
-            for k, cross in enumerate((cross_real, cross_imag)):
-                columns = jnp.concatenate(
-                    [cross[pl.ds(2 * n + m, BINS, stride=SB // 2), :].astype(jnp.bfloat16) for m in range(2)], axis=1
-                )
-                term = jnp.dot(lag_ref[k], columns, preferred_element_type=jnp.float32)
-                summed = term if summed is None else summed + term
-            turned = summed.T
+
+    def transforms(tile):
+        dft_copies[tile].wait()
+        bins = slice(tile * HT, (tile + 1) * HT)
+        for tile_pair in range(window_count * THEIRS // wide):
+            at = slice(tile_pair * wide, (tile_pair + 1) * wide)
+            spectra = [dot_nt(dft_ref[k, bins, : depth[k]], theirs[k, at, : depth[k]]) for k in range(4)]
+            for n in range(HT // strip):
+                for inner in range(wide // LANE):
+                    parts = [x[n * strip : (n + 1) * strip, inner * LANE : (inner + 1) * LANE] for x in spectra]
+                    power = sum(x * x for x in parts[1:]) + parts[0] * parts[0]
+                    level = jnp.sum(power, axis=0, keepdims=True)
+                    scale = lax.rsqrt(level * (1.0 / (2 * BAND)) + 1e-06)
+                    for parity in range(2):
+                        real, imag = parts[parity] * scale, parts[2 + parity] * scale
+
+                        def stacked(x, y):
+                            both = [v.reshape(strip // PACK, 1, PACK, LANE) for v in (x, y)]
+                            both = jnp.concatenate(both, axis=1).reshape(strip * 2, LANE)
+                            return both.astype(jnp.bfloat16)
+
+                        plain, crossed = stacked(real, imag), stacked(-imag, real)
+                        turned = pltpu.roll(jnp.where(first, crossed, plain), half, 1)
+                        for k, block in enumerate((jnp.where(first, plain, turned), jnp.where(first, turned, crossed))):
+                            w = (tile_pair * (wide // LANE) + inner) * 2 + k
+                            for m in range(strip // PACK):
+                                group = n * (strip // PACK) + m
+                                turn = group % slots // 2
+                                row = w // turns * LANE + (w + turn) % turns * 2 * PACK
+                                right[tile, parity * halves + group, row : row + 2 * PACK, :] = block[
+                                    m * 2 * PACK : (m + 1) * 2 * PACK
+                                ]
+
+        spectra = [dot_nt(own[k, :, : depth[k]], dft_ref[k, bins, : depth[k]]) for k in range(4)]
+        power = sum(x * x for x in spectra[1:]) + spectra[0] * spectra[0]
+        same = (
+            lax.broadcasted_iota(jnp.int32, (HT, HT), 0) // strip == lax.broadcasted_iota(jnp.int32, (HT, HT), 1) // strip
+        ).astype(jnp.float32).astype(jnp.bfloat16)
+        level = jnp.dot(power.astype(jnp.bfloat16), same, preferred_element_type=jnp.float32)
+        scale = lax.rsqrt(level * (1.0 / (2 * BAND)) + 1e-06)
+        for k in range(4):
+            white_own[tile, k] = (spectra[k] * scale).astype(jnp.bfloat16)
+
+        low_slot = lane // PACK % 2 == 0
+        for parity in range(2):
+            for part in range(HT // LANE):
+                for h in range(window_count // turns):
+                    moved = [[], []]
+                    for w in range(turns):
+                        row = (h * turns + w) * SB
+                        x = [
+                            white_own[tile, 2 * c + parity, row : row + SB, part * LANE : (part + 1) * LANE] for c in range(2)
+                        ]
+                        y = (
+                            jnp.where(low_slot, x[0], pltpu.roll(x[1], PACK, 1)),
+                            jnp.where(low_slot, pltpu.roll(x[0], LANE - PACK, 1), x[1]),
+                        )
+                        for k in range(2):
+                            moved[k].append(pltpu.roll(y[k], 2 * PACK * w, 1) if w else y[k])
+                    for slot in range(slots):
+                        turn, k = slot // 2, slot % 2
+                        joined = moved[k][0]
+                        for w in range(1, turns):
+                            joined = jnp.where(lane // (2 * PACK) == (turn + w) % turns, moved[k][w], joined)
+                        left[tile, parity * halves + part * slots + slot, h] = joined
+
+    def products(tile):
+        def several(n, carry):
+            one_group(tile, n)
+            return carry
+
+        lax.fori_loop(0, FT // PACK, several, 0, unroll=32)
+
+    for tile in range(TILES):
+        transforms(tile)
+        if tile:
+            products(tile - 1)
+    products(TILES - 1)
+
+    lag_copy.wait()
+    out_copies = []
+    for n in range(SB // 4):
+        summed = None
+        for k, cross in enumerate((cross_real, cross_imag)):
+            columns = jnp.concatenate(
+                [cross[pl.ds(2 * n + m, BINS, stride=SB // 2), :].astype(jnp.bfloat16) for m in range(2)], axis=1
+            )
+            term = jnp.dot(lag_ref[k], columns, preferred_element_type=jnp.float32)
+            summed = term if summed is None else summed + term
+        turned = summed.T
+        for h in range(2):
+            station = h * (SB // 2) + 2 * n
             for m in range(2):
-                for h in range(2):
-                    i = h * (SB // 2) + 2 * n + m
-                    for r in range(ROUNDS):
-                        row = ((m * 2 + h) * ROUNDS + r) * SB
-                        out_ref[r, pl.ds(pl.multiple_of(i * SB, SB), SB), :] = turned[row : row + SB]
-            return carry
-
-        lax.fori_loop(0, SB // 4, two_stations, 0, unroll=True)
+                for r in range(ROUNDS):
+                    row = ((m * 2 + h) * ROUNDS + r) * SB
+                    out_ref[r, (station + m) * SB : (station + m + 1) * SB, :] = turned[row : row + SB]
+            rows = slice(station * SB, (station + 2) * SB)
+            copy = pltpu.make_async_copy(
+                out_ref.at[:, rows, :], out_hbm.at[:, rows, :], out_sems.at[len(out_copies)]
+            )
+            copy.start()
+            out_copies.append(copy)
+    for copy in out_copies:
+        copy.wait()
 
 
 def correlate(window_starts, low, taper, dft, lag):
     window_count = window_starts.shape[0]
     planes = low.shape[0]
-    grid_spec = pltpu.PrefetchScalarGridSpec(
-        num_scalar_prefetch=1,
-        grid=(TILES,),
-        in_specs=[
-            pl.BlockSpec((planes, ROWS, LANE), lambda n, *_: (0, 0, 0)),
-            pl.BlockSpec((8, LANE), lambda n, *_: (0, 0)),
-            pl.BlockSpec(memory_space=pl.ANY),
-            pl.BlockSpec(memory_space=pl.ANY),
-        ],
-        out_specs=pl.BlockSpec((ROUNDS, SB * SB, LAGS), lambda n, *_: (0, 0, 0)),
+    in_vmem = pl.BlockSpec(memory_space=pltpu.VMEM)
+    anywhere = pl.BlockSpec(memory_space=pl.ANY)
+    return pl.pallas_call(
+        correlate_kernel,
+        in_specs=[pl.BlockSpec(memory_space=pltpu.SMEM), in_vmem, in_vmem, anywhere, anywhere],
+        out_specs=anywhere,
+        out_shape=jax.ShapeDtypeStruct((ROUNDS, SB * SB, LAGS), jnp.float32),
         scratch_shapes=[
+            pltpu.VMEM((ROUNDS, SB * SB, LAGS), jnp.float32),
             pltpu.VMEM(dft.shape, jnp.bfloat16),
             pltpu.VMEM(lag.shape, jnp.bfloat16),
             pltpu.VMEM((planes, ROWS, LANE), jnp.float32),
             pltpu.VMEM((planes, ROWS, LANE), jnp.float32),
             pltpu.VMEM((4, window_count * THEIRS, FOLD + LANE), jnp.bfloat16),
             pltpu.VMEM((4, window_count * SB, FOLD + LANE), jnp.bfloat16),
-            pltpu.VMEM((4, window_count * SB, HT), jnp.bfloat16),
-            pltpu.VMEM((FT // PACK, 2, SB, LANE), jnp.bfloat16),
-            pltpu.VMEM((FT // PACK, 2 * LANE, LANE), jnp.bfloat16),
+            pltpu.VMEM((TILES, 4, window_count * SB, HT), jnp.bfloat16),
+            pltpu.VMEM((TILES, FT // PACK, 2, SB, LANE), jnp.bfloat16),
+            pltpu.VMEM((TILES, FT // PACK, 2 * LANE, LANE), jnp.bfloat16),
             pltpu.VMEM((BINS * SB // 2, LANE), jnp.float32),
             pltpu.VMEM((BINS * SB // 2, LANE), jnp.float32),
             pltpu.SemaphoreType.DMA((TILES,)),
             pltpu.SemaphoreType.DMA,
+            pltpu.SemaphoreType.DMA((SB // 2,)),
         ],
-    )
-    return pl.pallas_call(
-        correlate_kernel,
-        grid_spec=grid_spec,
-        out_shape=jax.ShapeDtypeStruct((ROUNDS, SB * SB, LAGS), jnp.float32),
         compiler_params=pltpu.CompilerParams(vmem_limit_bytes=60 * 2**20),
     )(window_starts, low, taper, dft, lag)
 

time: 39.7 us -> 37.3 us (0.940)
  Pallas kernels: 39.5 us -> 37.1 us
    pallas_call x1, Pallas kernels: 17 us -> 14.5 us  [correlate(): pl.pallas_call(correlate_kernel, in_specs=[pl.BlockSpec(memory_space=pltp...]
where the time goes in v6:
time: 37.3 us; the launch traced here: 37.1 us
  Pallas kernels  37.1 us (99%)
    pallas_call x1, Pallas kernels, body(): pl.pallas_call(functools.partial(gather_kernel, members), out_shape=jax.S...  22.5 us
    pallas_call x1, Pallas kernels, correlate(): pl.pallas_call(correlate_kernel, in_specs=[pl.BlockSpec(memory_space=pltp...  14.5 us

profile of v6, /device:TPU:0, one launch (start us, length us, event | category | flops | bytes accessed | tf_op | source)
XLA Modules:
  0.0 37.1 jit_solution(2599458401561024767)
XLA Ops:
  0.0 22.5 %shard_map.82.low_ref = bf16[32,80,128]{2,1,0:T(8,128)(2,1)} custom-call(bf16[256,1024]{1,0:T(8,128)(2,1)} %raw_ref.1, bf16[256]{0:T(256)(128)(2,1)} %taps_ref.1, s32[1,256]{1,0:T(1,128)} %bitcast.2, s32[4,16]{1,0:T(4,128)} %pairing_ref.1), custom_call_target="tpu_custom_call" | custom-call | tf_op jit(solution)/shard_map/pallas_call | solution.py:537
  22.5 14.5 %shard_map.83 = f32[4,256,256]{2,1,0:T(8,128)} custom-call(s32[16]{0:T(128)} %starts_ref.1, bf16[32,80,128]{2,1,0:T(8,128)(2,1)} %shard_map.82.low_ref, f32[8,128]{1,0:T(8,128)} %constant.6.clone.taper_ref, bf16[4,512,640]{2,1,0:T(8,128)(2,1)} %constant.7.clone.dft_hbm, bf16[2,256,1024]{2,1,0:T(8,128)(2,1)} %constant.8.clone.lag_hbm), custom_call_target="tpu_custom_call" | custom-call | tf_op jit(solution)/shard_map/pallas_call | solution.py:504

commit v7 on v6

--- a/solution.py
+++ b/solution.py
@@ -119,6 +119,19 @@
     for peer in greeted:
         pl.semaphore_signal(barrier, inc=1, device_id={"sta": peer}, device_id_type=MESH)
 
+    relayed = line > 3
+    at_end = (rank == 0) | (rank == line - 1)
+    beside_end = (rank == 1) | (rank == line - 2)
+    joined = rank + jnp.where((rank == 0) | (rank == line - 2), 1, -1)
+    near_end = at_end | beside_end
+    if relayed:
+
+        @pl.when(near_end)
+        def _():
+            for n in range(1, QUAD):
+                peer = joined * QUAD + lax.rem(lead + n, QUAD)
+                pl.semaphore_signal(barrier, inc=1, device_id={"sta": peer}, device_id_type=MESH)
+
     mirror = (
         lax.broadcasted_iota(jnp.int32, (TAPS, TAPS), 0) + lax.broadcasted_iota(jnp.int32, (TAPS, TAPS), 1) == TAPS - 1
     ).astype(jnp.float32).astype(jnp.bfloat16)
@@ -141,7 +154,7 @@
         lane < half, spilled[: stations // 2], pltpu.roll(spilled[stations // 2 :], half, 1)
     ).astype(jnp.bfloat16)
 
-    pl.semaphore_wait(barrier, len(greeted))
+    pl.semaphore_wait(barrier, len(greeted) + (jnp.where(near_end, QUAD - 1, 0) if relayed else 0))
 
     halo_copy = pltpu.make_async_remote_copy(
         src_ref=tail,
@@ -178,28 +191,28 @@
 
     picks_sent = []
 
-    def share(source, piece, samples):
+    def share(source, piece, samples, peers, there):
         private[...] = samples.reshape(private.shape)
         plane = (source * QUAD + lead) * pieces + piece
-        for k, peer in enumerate(others + (me,)):
-            blocks = [pairing_ref[r, peer] for r in range(ROUNDS)] + [peer]
+        for peer in peers:
             slot = len(picks_sent)
-            for g, block in enumerate(blocks):
-                if k < len(others):
-                    picked[slot, g * SB : (g + 1) * SB, :] = private[block]
-                else:
-                    out_ref[plane, g * SB : (g + 1) * SB, :] = private[block]
-            if k < len(others):
-                copy = pltpu.make_async_remote_copy(
-                    src_ref=picked.at[slot],
-                    dst_ref=out_ref.at[plane],
-                    send_sem=pick_send.at[slot],
-                    recv_sem=pick_recv.at[plane],
-                    device_id={"sta": peer},
-                    device_id_type=MESH,
-                )
-                copy.start()
-                picks_sent.append(copy)
+            for g, block in enumerate([pairing_ref[r, peer] for r in range(ROUNDS)] + [peer]):
+                picked[slot, g * SB : (g + 1) * SB, :] = private[block]
+            copy = pltpu.make_async_remote_copy(
+                src_ref=picked.at[slot],
+                dst_ref=out_ref.at[plane],
+                send_sem=pick_send.at[slot],
+                recv_sem=pick_recv.at[plane],
+                device_id={"sta": peer},
+                device_id_type=MESH,
+            )
+            copy.start()
+            picks_sent.append(there)
+
+    def keep(source, piece):
+        plane = (source * QUAD + lead) * pieces + piece
+        for g, block in enumerate([pairing_ref[r, me] for r in range(ROUNDS)] + [me]):
+            out_ref[plane, g * SB : (g + 1) * SB, :] = private[block]
 
     def filtered(piece, first, spill=None):
         summed = lax.dot_general(
@@ -214,7 +227,8 @@
         column[rank, piece] = ordered
         pass_on(rank, piece, 1, rank < line - 1)
         pass_on(rank, piece, -1, rank > 0)
-        share(rank, piece, ordered)
+        share(rank, piece, ordered, others, None)
+        keep(rank, piece)
 
     for piece in range(pieces - 1, 0, -1):
         filtered(piece, piece * LANE * DEC - TAPS)
@@ -231,37 +245,77 @@
     spill = [jnp.where(lane < half, x, 0.0) for x in (spill, pltpu.roll(spill, half, 1))]
     filtered(0, -TAPS, jnp.concatenate(spill, axis=0))
 
-    for source, piece in expected:
+    for n, (source, piece) in enumerate(expected):
         from_below = source < rank
-        line_copy(source, piece, 0, source).wait_recv()
-        pass_on(
-            source,
-            piece,
-            jnp.where(from_below, 1, -1),
-            (from_below & (rank < line - 1)) | (jnp.logical_not(from_below) & (rank > 0)),
-        )
-        share(source, piece, column[source, piece])
+        there = (from_below & (rank < line - 1)) | (jnp.logical_not(from_below) & (rank > 0))
+        ahead = jnp.where(from_below, 1, -1)
+        if relayed and n >= len(expected) - pieces:
+            inside = jnp.logical_not(at_end)
+
+            @pl.when(inside)
+            def _():
+                line_copy(source, piece, 0, source).wait_recv()
+
+            pass_on(source, piece, ahead, there & jnp.logical_not(near_end))
+
+            @pl.when(beside_end)
+            def _():
+                ends = [joined * QUAD + lax.rem(lead + k, QUAD) for k in range(QUAD)]
+                share(source, piece, column[source, piece], ends, beside_end)
+
+            @pl.when(inside)
+            def _():
+                share(source, piece, column[source, piece], others, inside)
+                keep(source, piece)
+        else:
+            line_copy(source, piece, 0, source).wait_recv()
+            pass_on(source, piece, ahead, there)
+            share(source, piece, column[source, piece], others, None)
+            keep(source, piece)
+
+    def landed(plane):
+        pltpu.make_async_remote_copy(
+            src_ref=picked.at[0],
+            dst_ref=out_ref.at[plane],
+            send_sem=pick_send.at[0],
+            recv_sem=pick_recv.at[plane],
+            device_id={"sta": twin},
+            device_id_type=MESH,
+        ).wait_recv()
 
     for source in range(line):
         for piece in range(pieces):
             for peer in others:
-                plane = peer - rank * QUAD + source * QUAD
-                plane = plane * pieces + piece
-                pltpu.make_async_remote_copy(
-                    src_ref=picked.at[0],
-                    dst_ref=out_ref.at[plane],
-                    send_sem=pick_send.at[0],
-                    recv_sem=pick_recv.at[plane],
-                    device_id={"sta": twin},
-                    device_id_type=MESH,
-                ).wait_recv()
-    for copy in picks_sent:
-        copy.wait_send()
-    for copy, there in passed:
-
-        @pl.when(there)
+                landed((peer - rank * QUAD + source * QUAD) * pieces + piece)
+    if relayed:
+
+        @pl.when(at_end)
         def _():
+            for piece in range(pieces):
+                landed(((line - 1 - rank) * QUAD + lead) * pieces + piece)
+
+    leaving = [
+        (
+            pltpu.make_async_remote_copy(
+                src_ref=picked.at[slot],
+                dst_ref=out_ref.at[0],
+                send_sem=pick_send.at[slot],
+                recv_sem=pick_recv.at[0],
+                device_id={"sta": twin},
+                device_id_type=MESH,
+            ),
+            there,
+        )
+        for slot, there in enumerate(picks_sent)
+    ]
+    for copy, there in leaving + passed:
+        if there is None:
             copy.wait_send()
+        else:
+
+            @pl.when(there)
+            def _():
+                copy.wait_send()
 
     @pl.when(me < members - 1)
     def _():
@@ -550,12 +604,12 @@
             pltpu.VMEM((stations // 2, LANE), jnp.bfloat16),
             pltpu.VMEM((line, pieces, stations, LANE), jnp.bfloat16),
             pltpu.VMEM((stations // SB, SB, LANE), jnp.bfloat16),
-            pltpu.VMEM((3 * line * pieces, ROWS, LANE), jnp.bfloat16),
+            pltpu.VMEM(((3 * line + QUAD) * pieces, ROWS, LANE), jnp.bfloat16),
             pltpu.SemaphoreType.DMA,
             pltpu.SemaphoreType.DMA((2,)),
             pltpu.SemaphoreType.DMA(((line + 1) * pieces,)),
             pltpu.SemaphoreType.DMA((line * pieces,)),
-            pltpu.SemaphoreType.DMA((3 * line * pieces,)),
+            pltpu.SemaphoreType.DMA(((3 * line + QUAD) * pieces,)),
             pltpu.SemaphoreType.DMA((members * pieces,)),
         ],
         compiler_params=pltpu.CompilerParams(

time: 37.3 us -> 35.7 us (0.957)
  Pallas kernels: 37.1 us -> 35.5 us
    pallas_call x1, Pallas kernels: 22.5 us -> 21 us  [body(): pl.pallas_call(functools.partial(gather_kernel, members), out_shape=jax.S...]
where the time goes in v7:
time: 35.7 us; the launch traced here: 35.5 us
  Pallas kernels  35.5 us (99%)
    pallas_call x1, Pallas kernels, body(): pl.pallas_call(functools.partial(gather_kernel, members), out_shape=jax.S...  21 us
    pallas_call x1, Pallas kernels, correlate(): pl.pallas_call(correlate_kernel, in_specs=[pl.BlockSpec(memory_space=pltp...  14.5 us

profile of v7, /device:TPU:0, one launch (start us, length us, event | category | flops | bytes accessed | tf_op | source)
XLA Modules:
  0.0 35.5 jit_solution(7957577226652762924)
XLA Ops:
  0.0 21.0 %shard_map.82.low_ref = bf16[32,80,128]{2,1,0:T(8,128)(2,1)} custom-call(bf16[256,1024]{1,0:T(8,128)(2,1)} %raw_ref.1, bf16[256]{0:T(256)(128)(2,1)} %taps_ref.1, s32[1,256]{1,0:T(1,128)} %bitcast.2, s32[4,16]{1,0:T(4,128)} %pairing_ref.1), custom_call_target="tpu_custom_call" | custom-call | tf_op jit(solution)/shard_map/pallas_call | solution.py:591
  21.0 14.5 %shard_map.83 = f32[4,256,256]{2,1,0:T(8,128)} custom-call(s32[16]{0:T(128)} %starts_ref.1, bf16[32,80,128]{2,1,0:T(8,128)(2,1)} %shard_map.82.low_ref, f32[8,128]{1,0:T(8,128)} %constant.6.clone.taper_ref, bf16[4,512,640]{2,1,0:T(8,128)(2,1)} %constant.7.clone.dft_hbm, bf16[2,256,1024]{2,1,0:T(8,128)(2,1)} %constant.8.clone.lag_hbm), custom_call_target="tpu_custom_call" | custom-call | tf_op jit(solution)/shard_map/pallas_call | solution.py:558

commit v8 on v7

--- a/solution.py
+++ b/solution.py
@@ -79,6 +79,8 @@
     column,
     private,
     picked,
+    kept,
+    keep_sems,
     raw_sem,
     halo_sems,
     line_send,
@@ -209,10 +211,15 @@
             copy.start()
             picks_sent.append(there)
 
-    def keep(source, piece):
+    kept_there = []
+
+    def keep(source, piece, there):
+        slot = len(kept_there)
         plane = (source * QUAD + lead) * pieces + piece
         for g, block in enumerate([pairing_ref[r, me] for r in range(ROUNDS)] + [me]):
-            out_ref[plane, g * SB : (g + 1) * SB, :] = private[block]
+            kept[slot, g * SB : (g + 1) * SB, :] = private[block]
+        pltpu.make_async_copy(kept.at[slot], out_ref.at[plane], keep_sems.at[slot]).start()
+        kept_there.append(there)
 
     def filtered(piece, first, spill=None):
         summed = lax.dot_general(
@@ -228,7 +235,7 @@
         pass_on(rank, piece, 1, rank < line - 1)
         pass_on(rank, piece, -1, rank > 0)
         share(rank, piece, ordered, others, None)
-        keep(rank, piece)
+        keep(rank, piece, None)
 
     for piece in range(pieces - 1, 0, -1):
         filtered(piece, piece * LANE * DEC - TAPS)
@@ -266,12 +273,12 @@
             @pl.when(inside)
             def _():
                 share(source, piece, column[source, piece], others, inside)
-                keep(source, piece)
+                keep(source, piece, inside)
         else:
             line_copy(source, piece, 0, source).wait_recv()
             pass_on(source, piece, ahead, there)
             share(source, piece, column[source, piece], others, None)
-            keep(source, piece)
+            keep(source, piece, None)
 
     def landed(plane):
         pltpu.make_async_remote_copy(
@@ -308,6 +315,18 @@
         )
         for slot, there in enumerate(picks_sent)
     ]
+    def kept_done(slot):
+        pltpu.make_async_copy(kept.at[slot], out_ref.at[0], keep_sems.at[slot]).wait()
+
+    for slot, there in enumerate(kept_there):
+        if there is None:
+            kept_done(slot)
+        else:
+
+            @pl.when(there)
+            def _():
+                kept_done(slot)
+
     for copy, there in leaving + passed:
         if there is None:
             copy.wait_send()
@@ -597,7 +616,7 @@
             in_vmem,
             pl.BlockSpec(memory_space=pltpu.SMEM),
         ],
-        out_specs=in_vmem,
+        out_specs=pl.BlockSpec(memory_space=pl.ANY),
         scratch_shapes=[
             pltpu.VMEM((stations, local_time), jnp.bfloat16),
             pltpu.VMEM((stations // 2, LANE), jnp.bfloat16),
@@ -605,6 +624,8 @@
             pltpu.VMEM((line, pieces, stations, LANE), jnp.bfloat16),
             pltpu.VMEM((stations // SB, SB, LANE), jnp.bfloat16),
             pltpu.VMEM(((3 * line + QUAD) * pieces, ROWS, LANE), jnp.bfloat16),
+            pltpu.VMEM((line * pieces, ROWS, LANE), jnp.bfloat16),
+            pltpu.SemaphoreType.DMA((line * pieces,)),
             pltpu.SemaphoreType.DMA,
             pltpu.SemaphoreType.DMA((2,)),
             pltpu.SemaphoreType.DMA(((line + 1) * pieces,)),

time: 35.7 us -> 35.1 us (0.983)
  Pallas kernels: 35.5 us -> 34.9 us
    pallas_call x1, Pallas kernels: 21 us -> 20.3 us  [body(): pl.pallas_call(functools.partial(gather_kernel, members), out_shape=jax.S...]
where the time goes in v8:
time: 35.1 us; the launch traced here: 34.9 us
  Pallas kernels  34.9 us (99%)
    pallas_call x1, Pallas kernels, body(): pl.pallas_call(functools.partial(gather_kernel, members), out_shape=jax.S...  20.3 us
    pallas_call x1, Pallas kernels, correlate(): pl.pallas_call(correlate_kernel, in_specs=[pl.BlockSpec(memory_space=pltp...  14.5 us

profile of v8, /device:TPU:0, one launch (start us, length us, event | category | flops | bytes accessed | tf_op | source)
XLA Modules:
  0.0 34.9 jit_solution(1298112353070035190)
XLA Ops:
  0.0 20.3 %shard_map.82.low_ref = bf16[32,80,128]{2,1,0:T(8,128)(2,1)} custom-call(bf16[256,1024]{1,0:T(8,128)(2,1)} %raw_ref.1, bf16[256]{0:T(256)(128)(2,1)} %taps_ref.1, s32[1,256]{1,0:T(1,128)} %bitcast.2, s32[4,16]{1,0:T(4,128)} %pairing_ref.1), custom_call_target="tpu_custom_call" | custom-call | tf_op jit(solution)/shard_map/pallas_call | solution.py:610
  20.4 14.5 %shard_map.83 = f32[4,256,256]{2,1,0:T(8,128)} custom-call(s32[16]{0:T(128)} %starts_ref.1, bf16[32,80,128]{2,1,0:T(8,128)(2,1)} %shard_map.82.low_ref, f32[8,128]{1,0:T(8,128)} %constant.6.clone.taper_ref, bf16[4,512,640]{2,1,0:T(8,128)(2,1)} %constant.7.clone.dft_hbm, bf16[2,256,1024]{2,1,0:T(8,128)(2,1)} %constant.8.clone.lag_hbm), custom_call_target="tpu_custom_call" | custom-call | tf_op jit(solution)/shard_map/pallas_call | solution.py:577

commit v9 on v8

--- a/solution.py
+++ b/solution.py
@@ -96,7 +96,7 @@
     twin = me + turn
     across = rank * QUAD + lax.rem(lead + 2, QUAD)
     others = (across, across + turn, twin)
-    after, before = lax.rem(me + 1, members), lax.rem(me + members - 1, members)
+    after = lax.rem(me + 1, members)
 
     def of_rank(choose):
         chosen = choose(0)
@@ -117,9 +117,15 @@
     raw_copy.start()
 
     barrier = pltpu.get_barrier_semaphore()
-    greeted = [lax.rem(rank + n, line) * QUAD + lead for n in range(1, line)] + list(others) + [after, before]
-    for peer in greeted:
+    for peer in others:
         pl.semaphore_signal(barrier, inc=1, device_id={"sta": peer}, device_id_type=MESH)
+    greeters = len(others)
+    for ahead, there in ((QUAD, rank < line - 1), (-QUAD, rank > 0), (1, me < members - 1), (-1, me > 0)):
+        greeters = greeters + jnp.where(there, 1, 0)
+
+        @pl.when(there)
+        def _():
+            pl.semaphore_signal(barrier, inc=1, device_id={"sta": me + ahead}, device_id_type=MESH)
 
     relayed = line > 3
     at_end = (rank == 0) | (rank == line - 1)
@@ -156,7 +162,7 @@
         lane < half, spilled[: stations // 2], pltpu.roll(spilled[stations // 2 :], half, 1)
     ).astype(jnp.bfloat16)
 
-    pl.semaphore_wait(barrier, len(greeted) + (jnp.where(near_end, QUAD - 1, 0) if relayed else 0))
+    pl.semaphore_wait(barrier, greeters + (jnp.where(near_end, QUAD - 1, 0) if relayed else 0))
 
     halo_copy = pltpu.make_async_remote_copy(
         src_ref=tail,

time: 35.1 us -> 34.4 us (0.980)
  Pallas kernels: 34.9 us -> 34.2 us
    pallas_call x1, Pallas kernels: 20.3 us -> 19.6 us  [body(): pl.pallas_call(functools.partial(gather_kernel, members), out_shape=jax.S...]
where the time goes in v9:
time: 34.4 us; the launch traced here: 34.2 us
  Pallas kernels  34.2 us (99%)
    pallas_call x1, Pallas kernels, body(): pl.pallas_call(functools.partial(gather_kernel, members), out_shape=jax.S...  19.6 us
    pallas_call x1, Pallas kernels, correlate(): pl.pallas_call(correlate_kernel, in_specs=[pl.BlockSpec(memory_space=pltp...  14.5 us

profile of v9, /device:TPU:0, one launch (start us, length us, event | category | flops | bytes accessed | tf_op | source)
XLA Modules:
  0.0 34.2 jit_solution(18147282249519989106)
XLA Ops:
  0.0 19.6 %shard_map.82.low_ref = bf16[32,80,128]{2,1,0:T(8,128)(2,1)} custom-call(bf16[256,1024]{1,0:T(8,128)(2,1)} %raw_ref.1, bf16[256]{0:T(256)(128)(2,1)} %taps_ref.1, s32[1,256]{1,0:T(1,128)} %bitcast.2, s32[4,16]{1,0:T(4,128)} %pairing_ref.1), custom_call_target="tpu_custom_call" | custom-call | tf_op jit(solution)/shard_map/pallas_call | solution.py:616
  19.6 14.5 %shard_map.83 = f32[4,256,256]{2,1,0:T(8,128)} custom-call(s32[16]{0:T(128)} %starts_ref.1, bf16[32,80,128]{2,1,0:T(8,128)(2,1)} %shard_map.82.low_ref, f32[8,128]{1,0:T(8,128)} %constant.6.clone.taper_ref, bf16[4,512,640]{2,1,0:T(8,128)(2,1)} %constant.7.clone.dft_hbm, bf16[2,256,1024]{2,1,0:T(8,128)(2,1)} %constant.8.clone.lag_hbm), custom_call_target="tpu_custom_call" | custom-call | tf_op jit(solution)/shard_map/pallas_call | solution.py:583

commit v10 on v9

--- a/solution.py
+++ b/solution.py
@@ -397,7 +397,7 @@
         back[planes - 1 - n] = jnp.where(lane == 0, later, turned)
         return carry
 
-    lax.fori_loop(0, planes, one_plane, 0, unroll=16)
+    lax.fori_loop(0, planes, one_plane, 0, unroll=32)
 
     def one_window(w, carry):
         start = starts_ref[w]
@@ -441,7 +441,7 @@
             put(3, p, jnp.where(lane == 0, middle, summed) if p == 0 else summed)
         return carry
 
-    lax.fori_loop(0, window_count, one_window, 0, unroll=8)
+    lax.fori_loop(0, window_count, one_window, 0, unroll=16)
 
     def dot_nt(a, b):
         return lax.dot_general(a, b, NT, preferred_element_type=jnp.float32)

time: 34.4 us -> 35.3 us (1.026)
  Pallas kernels: 34.2 us -> 35 us
    pallas_call x1, Pallas kernels: 14.5 us -> 15.4 us  [correlate(): pl.pallas_call(correlate_kernel, in_specs=[pl.BlockSpec(memory_space=pltp...]
where the time goes in v10:
time: 35.3 us; the launch traced here: 35.1 us
  Pallas kernels  35 us (99%)
    pallas_call x1, Pallas kernels, body(): pl.pallas_call(functools.partial(gather_kernel, members), out_shape=jax.S...  19.6 us
    pallas_call x1, Pallas kernels, correlate(): pl.pallas_call(correlate_kernel, in_specs=[pl.BlockSpec(memory_space=pltp...  15.4 us

profile of v10, /device:TPU:0, one launch (start us, length us, event | category | flops | bytes accessed | tf_op | source)
XLA Modules:
  0.0 35.1 jit_solution(12824901681991251526)
XLA Ops:
  0.0 19.6 %shard_map.82.low_ref = bf16[32,80,128]{2,1,0:T(8,128)(2,1)} custom-call(bf16[256,1024]{1,0:T(8,128)(2,1)} %raw_ref.1, bf16[256]{0:T(256)(128)(2,1)} %taps_ref.1, s32[1,256]{1,0:T(1,128)} %bitcast.2, s32[4,16]{1,0:T(4,128)} %pairing_ref.1), custom_call_target="tpu_custom_call" | custom-call | tf_op jit(solution)/shard_map/pallas_call | solution.py:616
  19.6 15.4 %shard_map.83 = f32[4,256,256]{2,1,0:T(8,128)} custom-call(s32[16]{0:T(128)} %starts_ref.1, bf16[32,80,128]{2,1,0:T(8,128)(2,1)} %shard_map.82.low_ref, f32[8,128]{1,0:T(8,128)} %constant.6.clone.taper_ref, bf16[4,512,640]{2,1,0:T(8,128)(2,1)} %constant.7.clone.dft_hbm, bf16[2,256,1024]{2,1,0:T(8,128)(2,1)} %constant.8.clone.lag_hbm), custom_call_target="tpu_custom_call" | custom-call | tf_op jit(solution)/shard_map/pallas_call | solution.py:583
